TPU v7x, 512 devices: a whole 4x4x16 slice. The times are simulated.
512 devices in a mesh: ctx: 32 (over y_hi, z), tp: 16 (over x, y_lo, core).
Axes of the slice: x: 4, y: 4 (y_hi: 2, y_lo: 2; y = y_hi * 2 + y_lo), z: 16, core: 2. Of those that a mesh axis runs over, the one named last changes fastest.
Arguments:
- query_proj: bfloat16 [4096, 4096], P('ctx', 'tp'), may hold values from -64 to 64
- key_proj: bfloat16 [4096, 1024], P('ctx'), may hold values from -64 to 64
- value_proj: bfloat16 [4096, 1024], P('ctx'), may hold values from -6 to 6
- residual: bfloat16 [4096, 5120], P('ctx', 'tp'), may hold values from -6 to 6
- out_weight: bfloat16 [4096, 5120], P('tp', 'ctx'), may hold values from -0.1875 to 0.1875
- norm_gain: bfloat16 [5120], P('tp'), may hold values from 0.25 to 1.75
- mlp_weight: bfloat16 [5120, 5120], P('ctx', 'tp'), may hold values from -0.078125 to 0.078125
- level_weight: bfloat16 [5120, 128], P('tp'), may hold values from -0.078125 to 0.078125
- step_positions: int32 [1024], replicated, may hold values from 0 to 4095, as said below
Outputs:
- attended: bfloat16 [4096, 4096], P('ctx', 'tp')
- step_states: bfloat16 [1024, 5120], P('ctx', 'tp')
- step_levels: float32 [1024, 128], P('ctx', 'tp')
Inputs may be any that keep to these rules, and one draw needn't show every extreme that they name: `step_positions`: 1024 distinct increasing positions; the 128 rows of one index of ctx hold at most 128 of them, and some index holds exactly that many.
All inputs are finite; a program needn't handle non-finite values.
Results may differ from a plain program's by a relative error of at most 0.013.
Values may be sent and summed in bfloat16 or wider, within the bound.
A program may use at most 64 MiB of HBM per device.

v0:
```python
import jax
import jax.numpy as jnp
from jax import lax
from jax.sharding import PartitionSpec as P

D = 5120
KVH = 8
HD = 128
QH = 32


masked_score = -1e30


def update_half(state, query_half, spots, key_piece, value_piece, group_count, scale):
    highest, totals, accum = state
    length = key_piece.shape[0]
    keys_split = key_piece.reshape(length, group_count, HD)
    values_split = value_piece.reshape(length, group_count, HD)
    scores = (
        jnp.einsum("qkgd,pkd->kgqp", query_half, keys_split, preferred_element_type=jnp.float32)
        * scale
    )
    key_spots = jnp.arange(length, dtype=jnp.int32)
    allowed = key_spots[None, :] <= spots[:, None]
    scores = jnp.where(allowed, scores, masked_score)
    new_highest = jnp.maximum(highest, jnp.max(scores, axis=-1))
    weights = jnp.where(allowed, jnp.exp(scores - new_highest[..., None]), 0.0)
    totals = jnp.sum(weights, axis=-1)
    accum = jnp.einsum(
        "kgqp,pkd->kgqd",
        weights.astype(jnp.bfloat16),
        values_split,
        preferred_element_type=jnp.float32,
    )
    return (new_highest, totals, accum)


def on_device(
    query_proj,
    key_proj,
    value_proj,
    residual,
    out_weight,
    norm_gain,
    mlp_weight,
    level_weight,
    step_positions,
):
    rows = query_proj.shape[0]
    middle = rows // 2
    ctx_count = lax.axis_size("ctx")
    ctx_index = lax.axis_index("ctx")
    tp_index = lax.axis_index("tp")
    heads_here = query_proj.shape[1] // HD
    group = QH // KVH
    group_count = max(1, heads_here // group)
    per_group = heads_here // group_count
    first_group = tp_index * heads_here // group
    key_mine = lax.dynamic_slice_in_dim(key_proj, first_group * HD, group_count * HD, 1)
    value_mine = lax.dynamic_slice_in_dim(value_proj, first_group * HD, group_count * HD, 1)
    scale = HD ** (-0.5)
    base = ctx_index * rows
    held_spots = base + jnp.arange(rows, dtype=jnp.int32)
    spot_pair = (held_spots[:middle], held_spots[middle:])
    query_pair = (
        query_proj[:middle].reshape(middle, group_count, per_group, HD),
        query_proj[middle:].reshape(middle, group_count, per_group, HD),
    )
    last_spots = (spot_pair[0][middle - 1], spot_pair[1][middle - 1])

    def empty_state():
        return (
            jnp.full((group_count, per_group, middle), masked_score, jnp.float32),
            jnp.zeros((group_count, per_group, middle), jnp.float32),
            jnp.zeros((group_count, per_group, middle, HD), jnp.float32),
        )

    carry = (empty_state(), empty_state())
    start = jnp.int32(0)
    key_piece = lax.all_gather(key_mine, "ctx", axis=0, tiled=True)
    value_piece = lax.all_gather(value_mine, "ctx", axis=0, tiled=True)
    updated = []
    for which in range(2):

        def advance(state, which=which):
            return update_half(
                state,
                query_pair[which],
                spot_pair[which],
                key_piece,
                value_piece,
                group_count,
                scale,
            )

        def keep(state):
            return state

        updated.append(lax.cond(start <= last_spots[which], advance, keep, carry[which]))
    final = (updated[0], updated[1])
    outputs = []
    for highest, totals, accum in final:
        mixed = accum / totals[..., None]
        outputs.append(
            mixed.transpose(2, 0, 1, 3).reshape(middle, heads_here * HD).astype(jnp.bfloat16)
        )
    held_out = jnp.concatenate(outputs, axis=0)
    count = step_positions.shape[0]
    steps_here = count // ctx_count
    slots_each = 4 * steps_here // ctx_count
    owners = jnp.arange(ctx_count, dtype=jnp.int32)[:, None]
    slot_index = jnp.arange(slots_each, dtype=jnp.int32)[None, :]
    first_step = jnp.sum((step_positions < base).astype(jnp.int32))
    end_step = jnp.sum((step_positions < base + rows).astype(jnp.int32))
    chosen = first_step + (owners - first_step) % ctx_count + slot_index * ctx_count
    present = (chosen < end_step).reshape(-1, 1)
    local_rows = step_positions[jnp.minimum(chosen, count - 1)].reshape(-1) - base
    local_rows = jnp.where(present[:, 0], local_rows, 0)
    send_attended = jnp.where(present, held_out[local_rows], jnp.zeros((), jnp.bfloat16)).reshape(
        ctx_count, slots_each, -1
    )
    send_residual = jnp.where(present, residual[local_rows], jnp.zeros((), jnp.bfloat16)).reshape(
        ctx_count, slots_each, -1
    )
    got_attended, got_residual = (
        lax.all_to_all(send_attended, "ctx", split_axis=0, concat_axis=0, tiled=True),
        lax.all_to_all(send_residual, "ctx", split_axis=0, concat_axis=0, tiled=True),
    )
    owned = jnp.arange(steps_here, dtype=jnp.int32) * ctx_count + ctx_index
    owned_spots = step_positions[owned]
    source = owned_spots // rows
    source_first = jnp.sum(
        (step_positions[None, :] < (source * rows)[:, None]).astype(jnp.int32), axis=1
    )
    rank = (owned - source_first) // ctx_count
    pick = source * slots_each + rank
    step_attended = got_attended.reshape(ctx_count * slots_each, -1)[pick]
    step_residual = got_residual.reshape(ctx_count * slots_each, -1)[pick]
    partial_terms = jnp.dot(
        step_attended,
        lax.all_gather(out_weight, "ctx", axis=1, tiled=True),
        preferred_element_type=jnp.float32,
    )
    projected = lax.psum_scatter(
        partial_terms.astype(jnp.bfloat16), "tp", scatter_dimension=1, tiled=True
    ).astype(jnp.float32)
    step_states = (step_residual.astype(jnp.float32) + projected).astype(jnp.bfloat16)
    states_wide = step_states.astype(jnp.float32)
    squares = lax.psum(jnp.sum(states_wide * states_wide, axis=-1), "tp")
    factor = lax.rsqrt(squares / D + 1e-06)[:, None]
    normed_local = (states_wide * factor * norm_gain.astype(jnp.float32)).astype(jnp.bfloat16)
    normed = lax.all_gather(normed_local, "tp", axis=1, tiled=True)
    pre = jnp.dot(
        normed,
        lax.all_gather(mlp_weight, "ctx", axis=0, tiled=True),
        preferred_element_type=jnp.float32,
    )
    hidden = jax.nn.silu(pre).astype(jnp.bfloat16)
    level_terms = jnp.dot(hidden, level_weight, preferred_element_type=jnp.float32)
    step_levels = lax.psum_scatter(level_terms, "tp", scatter_dimension=1, tiled=True)
    return (held_out, step_states, step_levels)


def solution(mesh):
    in_specs = (
        P("ctx", "tp"),
        P("ctx", None),
        P("ctx", None),
        P("ctx", "tp"),
        P("tp", "ctx"),
        P("tp"),
        P("ctx", "tp"),
        P("tp", None),
        P(),
    )
    out_specs = (P("ctx", "tp"), P("ctx", "tp"), P("ctx", "tp"))
    return jax.shard_map(
        on_device, mesh=mesh, in_specs=in_specs, out_specs=out_specs, check_vma=False
    )
```

profile of v0, /device:TPU:1, one launch (start us, length us, event | category | flops | bytes accessed | tf_op | source)
XLA Modules:
  0.0 743.3 jit_solution(5762425692753296062)
XLA Ops:
  7.3 0.9 copy-done
  8.1 0.6 constant_dynamic-slice_fusion.2
  8.8 1.4 constant_dynamic-slice_fusion.1
  10.3 0.7 all-gather.10.cloned.1.call-update
  11.0 1.3 convert_reduce_fusion.1
  12.3 0.7 fusion.36
  13.2 1.0 gather_fusion
  14.2 0.6 fusion.45
  16.1 0.7 broadcast_select_fusion.2
  16.9 0.7 gather_fusion.2
  17.6 0.2 convert_reduce_fusion
  17.8 0.7 add_compare_fusion
  18.5 132.3 %all-gather.6.cloned.1.call-done = bf16[4096,128]{1,0:T(8,128)(2,1)} async-done(((bf16[128,128]{1,0:T(8,128)(2,1)}), bf16[4096,128]{1,0:T(8,128)(2,1)}) %all-gather.6.cloned.1.call-update) | async-done | bytes 1048592 | tf_op jit(solution)/shard_map/all_gather | solution.py:81
  150.9 140.3 %all-gather.8.cloned.1.call-done = bf16[4096,128]{1,0:T(8,128)(2,1)} async-done(((bf16[128,128]{1,0:T(8,128)(2,1)}), bf16[4096,128]{1,0:T(8,128)(2,1)}) %all-gather.8.cloned.1.call-update) | async-done | bytes 1048592 | tf_op jit(solution)/shard_map/all_gather | solution.py:82
  291.2 3.5 conditional.3
  291.3 0.2 iota_compare_fusion.1
  291.5 1.9 fusion.44
  293.4 0.6 convolution_bitcast_fusion.1
  294.1 0.7 fusion.17
  294.9 3.5 conditional.2
  294.9 0.2 iota_compare_fusion
  295.1 1.9 fusion.43
  297.0 0.6 convolution_bitcast_fusion
  297.7 0.7 fusion.3
  298.5 0.8 gather_fusion.4
  299.4 0.7 broadcast_select_fusion.1
  300.1 7.3 all-to-all-start.1
  307.5 14.7 %all-to-all-done.1 = bf16[32,4,256]{2,1,0:T(4,128)(2,1)S(1)} async-done(((bf16[32,4,256]{2,1,0:T(4,128)(2,1)}), bf16[32,4,256]{2,1,0:T(4,128)(2,1)S(1)}, u32[]{:S(2)}, u32[]{:S(2)}) %all-to-all-start.1) | async-done | bytes 65568 | tf_op jit(solution)/shard_map/all_to_all | solution.py:127
  322.2 0.6 gather_fusion.5
  322.8 119.7 %all-gather.10.cloned.1.call-done = bf16[256,5120]{0,1:T(8,128)(2,1)} async-done(((bf16[256,160]{0,1:T(8,128)(2,1)}), bf16[256,5120]{0,1:T(8,128)(2,1)}) %all-gather.10.cloned.1.call-update) | async-done | bytes 2621456 | tf_op jit(solution)/shard_map/all_gather | solution.py:142
  442.5 2.6 convolution_convert_fusion
  445.2 1.4 copy.33
  446.6 0.5 all-gather.12.cloned.1.call-update
  447.3 0.9 gather_fusion.1
  448.2 0.8 broadcast_select_fusion
  449.0 7.4 %all-to-all-start = ((bf16[32,4,320]{2,1,0:T(4,128)(2,1)}), bf16[32,4,320]{2,1,0:T(4,128)(2,1)S(1)}, u32[]{:S(2)}, u32[]{:S(2)}) async-start(bf16[32,4,320]{2,1,0:T(4,128)(2,1)} %broadcast_select_fusion), calls=%async_computation | async-start | bytes 196608 | tf_op jit(solution)/shard_map/all_to_all | solution.py:128
  456.5 1.3 dynamic-slice
  458.4 13.4 %all-to-all-done = bf16[32,4,320]{2,1,0:T(4,128)(2,1)S(1)} async-done(((bf16[32,4,320]{2,1,0:T(4,128)(2,1)}), bf16[32,4,320]{2,1,0:T(4,128)(2,1)S(1)}, u32[]{:S(2)}, u32[]{:S(2)}) %all-to-all-start) | async-done | bytes 81952 | tf_op jit(solution)/shard_map/all_to_all | solution.py:128
  471.9 0.6 gather_fusion.3
  472.5 45.3 %reduce-scatter.4.cloned.1.call-done = bf16[320,32]{1,0:T(8,128)(2,1)} async-done(((bf16[5120,32]{1,0:T(8,128)(2,1)}), bf16[320,32]{1,0:T(8,128)(2,1)}) %reduce-scatter.4.cloned.1.call-update) | async-done | bytes 20496
  517.8 1.0 copy.34
  518.9 29.9 %psum.7 = f32[32]{0:T(128)S(1)} all-reduce(f32[32]{0:T(128)S(1)} %get-tuple-element.43), channel_id=1, replica_groups=mesh['ctx'=32,'tp'=16] {'tp'}, use_global_device_ids=true, to_apply=%region_13.14 | all-reduce | flops 32 | bytes 256 | tf_op jit(solution)/shard_map/psum | solution.py:150
  548.9 18.7 %all-gather = bf16[16,320,32]{1,2,0:T(8,128)(2,1)S(1)} all-gather(bf16[1,320,32]{1,2,0:T(8,128)(2,1)S(1)} %fusion.34), channel_id=1, replica_groups=mesh['ctx'=32,'tp'=16] {'tp'}, dimensions={0}, use_global_device_ids=true | all-gather | bytes 348160 | tf_op jit(solution)/shard_map/all_gather | solution.py:153
  567.8 0.3 reshape.447
  568.1 108.2 %all-gather.12.cloned.1.call-done = bf16[5120,320]{1,0:T(8,128)(2,1)} async-done(((bf16[160,320]{1,0:T(8,128)(2,1)}), bf16[5120,320]{1,0:T(8,128)(2,1)}) %all-gather.12.cloned.1.call-update) | async-done | bytes 3276816 | tf_op jit(solution)/shard_map/all_gather | solution.py:156
  676.2 3.0 fusion.33
  679.2 56.9 %all-reduce = f32[32,128]{0,1:T(8,128)S(1)} all-reduce(f32[32,128]{0,1:T(8,128)S(1)} %fusion.33), channel_id=3, replica_groups=mesh['ctx'=32,'tp'=16] {'tp'}, use_global_device_ids=true, to_apply=%region_14.15.clone | all-reduce | flops 4096 | bytes 32768
  736.2 0.6 constant_dynamic-slice_fusion
  (60 shorter events, 1.7 us)
Async XLA Ops:
  7.2 1.0 copy-start
  7.2 6.0 copy-start.1
  7.2 143.7 %all-gather.6.cloned.1.call-start = ((), (), s32[]{:S(2)}) async-start(), calls=%async_computation.3 | async-start | bytes 1081344 | tf_op jit(solution)/shard_map/all_gather | solution.py:81
  8.8 282.5 %all-gather.8.cloned.1.call-start = ((), (), s32[]{:S(2)}) async-start(), calls=%async_computation.4 | async-start | bytes 1081344 | tf_op jit(solution)/shard_map/all_gather | solution.py:82
  10.2 432.3 %all-gather.10.cloned.1.call-start = ((), (), s32[]{:S(2)}) async-start(), calls=%async_computation.5 | async-start | bytes 2703360 | tf_op jit(solution)/shard_map/all_gather | solution.py:142
  13.2 278.1 %copy-start.6 = (bf16[128,256]{1,0:T(8,128)(2,1)S(1)}, bf16[128,256]{1,0:T(8,128)(2,1)}, u32[]{:S(2)}) copy-start(bf16[128,256]{1,0:T(8,128)(2,1)} %param.13) | copy-start | bytes 196612
  291.2 2.2 copy-start.8
  294.9 2.1 copy-start.9
  298.5 146.7 %copy-start.2 = (bf16[128,256]{1,0:T(8,128)(2,1)}, bf16[128,256]{1,0:T(8,128)(2,1)S(1)}, u32[]{:S(2)}) copy-start(bf16[128,256]{1,0:T(8,128)(2,1)S(1)} %bitcast_dynamic-update-slice_fusion) | copy-start | bytes 196612
  300.1 22.0 %all-to-all-start.1 = ((bf16[32,4,256]{2,1,0:T(4,128)(2,1)}), bf16[32,4,256]{2,1,0:T(4,128)(2,1)S(1)}, u32[]{:S(2)}, u32[]{:S(2)}) async-start(bf16[32,4,256]{2,1,0:T(4,128)(2,1)} %broadcast_select_fusion.1), calls=%async_computation.1 | async-start | bytes 131072 | tf_op jit(solution)/shard_map/all_to_all | solution.py:127
  307.4 210.4 %reduce-scatter.4.cloned.1.call-start = ((), (), s32[]{:S(2)}) async-start(), calls=%async_computation.7 | async-start | bytes 1392640
  445.2 2.0 copy-start.4
  445.2 11.3 %copy-start.7 = (bf16[320]{0:T(512)(128)(2,1)S(1)}, bf16[320]{0:T(512)(128)(2,1)}, u32[]{:S(2)}) copy-start(bf16[320]{0:T(512)(128)(2,1)} %param.18) | copy-start | bytes 1924
  446.6 229.6 %all-gather.12.cloned.1.call-start = ((), (), s32[]{:S(2)}) async-start(), calls=%async_computation.6 | async-start | bytes 4055040 | tf_op jit(solution)/shard_map/all_gather | solution.py:156
  447.2 229.0 %copy-start.5 = (bf16[320,128]{1,0:T(8,128)(2,1)S(1)}, bf16[320,128]{1,0:T(8,128)(2,1)}, u32[]{:S(2)}) copy-start(bf16[320,128]{1,0:T(8,128)(2,1)} %param.20) | copy-start | bytes 245764
  449.0 22.8 %all-to-all-start = ((bf16[32,4,320]{2,1,0:T(4,128)(2,1)}), bf16[32,4,320]{2,1,0:T(4,128)(2,1)S(1)}, u32[]{:S(2)}, u32[]{:S(2)}) async-start(bf16[32,4,320]{2,1,0:T(4,128)(2,1)} %broadcast_select_fusion), calls=%async_computation | async-start | bytes 196608 | tf_op jit(solution)/shard_map/all_to_all | solution.py:128
  518.9 160.3 %copy-start.3 = (bf16[32,320]{1,0:T(8,128)(2,1)}, bf16[32,320]{1,0:T(8,128)(2,1)S(1)}, u32[]{:S(2)}) copy-start(bf16[32,320]{1,0:T(8,128)(2,1)S(1)} %get-tuple-element.44) | copy-start | bytes 61444
Sparse Core Ops, SparseCore 0:
  11.7 139.1 all-gather.5
  154.0 137.1 all-gather.7
  294.3 148.1 all-gather.9
  446.7 71.0 reduce-scatter.3
  520.7 155.4 all-gather.11
where the time goes:
time: 747 us; the launch traced here: 743 us
  waiting for transfers between devices  575 us (77%)
  blocking collectives  106 us (14%)
  between operations  16 us (2%)
  starting transfers between devices  14.9 us (2%)
  local copies, waits for them, and re-layouts  13.5 us (2%)
  matrix products  10.6 us (1%)
    all_gather x1, waiting for transfers between devices, on_device(): value_piece = lax.all_gather(value_mine, 'ctx', axis=0, tiled=True)  140 us
    all_gather x1, waiting for transfers between devices, on_device(): key_piece = lax.all_gather(key_mine, 'ctx', axis=0, tiled=True)  132 us
    all_gather x1, waiting for transfers between devices, on_device(): lax.all_gather(out_weight, 'ctx', axis=1, tiled=True)  120 us
    all_gather x1, waiting for transfers between devices, on_device(): lax.all_gather(mlp_weight, 'ctx', axis=0, tiled=True)  108 us
    unnamed x1, blocking collectives  56.9 us
    unnamed x6, waiting for transfers between devices  46.5 us
    psum x1, blocking collectives, on_device(): squares = lax.psum(jnp.sum(states_wide * states_wide, axis=-1), 'tp')  29.9 us
    all_gather x1, blocking collectives, on_device(): normed = lax.all_gather(normed_local, 'tp', axis=1, tiled=True)  18.7 us
  transfers between devices with their start and end apart: 7, of which 7 were waited for; matrix products, arithmetic and copies ran while one was open for 3% of the time, Pallas kernels for 0%

commit v1 on v0

v1 whole, which is shorter than its diff:
```python
import functools

import jax
import jax.numpy as jnp
from jax import lax
from jax.experimental import pallas as pl
from jax.experimental.pallas import tpu as pltpu
from jax.sharding import PartitionSpec as P

D = 5120
HD = 128
TOK = 128
STEPS = 32
COLS = 640
MASKED = -1e30
MESH = pl.DeviceIdType.MESH
F32 = jnp.float32
BF16 = jnp.bfloat16
I32 = jnp.int32
NEAR = (0, -1, 1, -2)


def iota(shape, dim):
    return lax.broadcasted_iota(I32, shape, dim)


def nn(a, b):
    return lax.dot_general(a, b, (((1,), (0,)), ((), ())), preferred_element_type=F32)


def nt(a, b):
    return lax.dot_general(a, b, (((1,), (1,)), ((), ())), preferred_element_type=F32)


def tn(a, b):
    return lax.dot_general(a, b, (((0,), (0,)), ((), ())), preferred_element_type=F32)


def shift(rows, cols, offset):
    return (iota((rows, cols), 0) + offset == iota((rows, cols), 1)).astype(BF16)


def kernel(
    q_ref, k_ref, v_ref, res_ref, wo_ref, gain_ref, wm_ref, lw_ref, pos_ref,
    att_ref, states_ref, levels_ref,
    kv, qall, qsend, qrecv, qmid_s, qmid_r, posc,
    rsend, rbuf, gbuf, wob, wmb, wobig, wmbig, lwt,
    agrp, pb, rb, sb, ob_s, ob, yb, yr, fb, fr,
    far_s, far_r, near_s, near_r, y_s, y_r, c_s, c_r,
    q_s, q_r, qm_s, qm_r, r_s, r_r, g_s, g_r, w_s, w_r,
    a_s, a_r, p_s, p_r, s_s, s_r, o_s, o_r, z_s, z_r, f_s, f_r,
):
    c = lax.axis_index("ctx")
    t = lax.axis_index("tp")
    z = lax.rem(c, 16)
    yh = c // 16
    core = lax.rem(t, 2)
    group = t // 2
    par = lax.rem(z, 2)
    mate_z = z + 1 - 2 * par
    pair = z // 2
    zr = lax.rem(z, 4)
    zq = z // 4
    partner = ((1 - yh) * 16 + z, t)
    other_core = (c, t + 1 - 2 * core)
    sends = []

    def zdev(d):
        return (yh * 16 + lax.rem(z + 16 + d, 16), t)

    def tdev(d):
        return (c, lax.rem(t + d, 16))

    def send(src, dst, ssem, rsem, dev):
        copy = pltpu.make_async_remote_copy(
            src_ref=src, dst_ref=dst, send_sem=ssem, recv_sem=rsem, device_id=dev, device_id_type=MESH
        )
        copy.start()
        sends.append(copy)

    def arrived(dst, rsem):
        pltpu.make_async_copy(dst, dst, rsem).wait()

    barrier = pltpu.get_barrier_semaphore()

    def greet(dev):
        pl.semaphore_signal(barrier, inc=1, device_id=dev, device_id_type=MESH)

    for d in range(1, 16):
        greet(zdev(d))
        greet(tdev(d))
    greet(partner)
    greet(((1 - yh) * 16 + mate_z, t))
    is_self = lax.rem(t, 8) == pair
    for y in range(2):
        for p in range(2):
            for j in range(2):
                dev = (y * 16 + 2 * lax.rem(t, 8) + p, j * 8 + pair)

                @pl.when(jnp.logical_not((dev[0] == c) & (dev[1] == t)))
                def _(dev=dev):
                    greet(dev)

    pos8 = pos_ref[...]
    hi8 = (pos8 >> 6).astype(F32).astype(BF16)
    lo8 = (pos8 & 63).astype(F32).astype(BF16)
    eye128 = shift(128, 128, 0)
    post = (nt(eye128, hi8) * 64.0 + nt(eye128, lo8)).astype(I32)
    base = c * TOK

    def before(limit):
        hits = jnp.where(pos8 < limit, 1.0, 0.0)
        return jnp.sum(jnp.sum(hits, axis=1, keepdims=True), axis=0, keepdims=True).astype(I32)

    first = before(base)
    selq = jnp.zeros((256, TOK), F32)
    selr = jnp.zeros((128, TOK), F32)
    lane_q = iota((128, 256), 1)
    owner_q = ((lane_q >> 3) & 1) * 16 + (lane_q >> 4)
    lane_r = iota((128, 128), 1)
    owner_r = (lane_r >> 6) * 16 + ((lane_r >> 2) & 7) * 2 + ((lane_r >> 5) & 1)
    for a in range(8):
        col = post[:, a : a + 1]
        step = iota((128, 1), 0) + a * 128
        rank = jnp.where((col >= base) & (col < base + TOK), (step - first) >> 5, 1000)
        owner = step & 31
        held = (col == iota((128, TOK), 1) + base).astype(BF16)
        selq += tn(((owner == owner_q) & (rank == (lane_q & 3))).astype(BF16), held)
        selr += tn(((owner == owner_r) & (rank == (lane_r & 3))).astype(BF16), held)
    selq = selq.astype(BF16)
    head_row = (iota((256, 128), 0) >> 2) & 1
    qsend[...] = jnp.where(head_row == 0, nn(selq, q_ref[:, :HD]), nn(selq, q_ref[:, HD:])).astype(BF16)
    rsend[...] = nn(selr.astype(BF16), res_ref[...]).astype(BF16)
    lanes = pl.ds(pl.multiple_of(group * HD, HD), HD)
    kv[core, yh, zr, zq] = jnp.where(core == 0, k_ref[:, lanes], v_ref[:, lanes])
    qall[0:TOK] = q_ref[:, :HD]
    qall[160 : 160 + TOK] = q_ref[:, HD:]

    def rows_of(count, owner):
        pick = ((iota((count, 8), 0) & 31) >> 2 == iota((count, 8), 1)).astype(BF16)
        spread = nn(pick, hi8) * 64.0 + nn(pick, lo8)
        lane = (iota((count, 128), 0) & 3) * 32 + owner
        return jnp.sum(jnp.where(iota((count, 128), 1) == lane, spread, 0.0), axis=1, keepdims=True)

    mine = rows_of(STEPS, c)
    for h in range(2):
        posc[h * 160 : h * 160 + TOK] = iota((TOK, 128), 0) + base
        posc[h * 160 + TOK : (h + 1) * 160] = jnp.broadcast_to(mine.astype(I32), (STEPS, 128))

    pl.semaphore_wait(barrier, jnp.where(is_self, 39, 40))

    here = kv.at[core, yh, zr, zq]
    for f in (2, 1, 3):
        send(here, here, far_s.at[f], far_r.at[f], zdev(4 * f))
    for d in (8, 7, 9, 6, 10, 5, 11, 4, 12, 3, 13, 2, 14, 1, 15):
        zd = lax.rem(z + d, 16)
        send(
            qsend.at[pl.ds(zd * 16, 16)], qrecv.at[pl.ds(z * 16, 16)], q_s.at[d], q_r.at[d], zdev(d)
        )
    qrecv[pl.ds(pl.multiple_of(z * 16, 16), 16)] = qsend[pl.ds(pl.multiple_of(z * 16, 16), 16)]

    def near_block(f):
        block = kv.at[core, yh, zr, lax.rem(zq + 4 - f, 4)]
        if f:
            arrived(block, far_r.at[f])
        for n in (3, 1, 2):
            send(block, block, near_s.at[n, f], near_r.at[n, f], zdev(-NEAR[n]))

    near_block(0)
    half_t = t // 8
    for g in range(4):
        dev = ((g // 2) * 16 + 2 * lax.rem(t, 8) + g % 2, yh * 8 + pair)
        src = rsend.at[pl.ds(g * 32, 32)]
        dst = rbuf.at[half_t, par]
        own = (dev[0] == c) & (dev[1] == t)

        @pl.when(own)
        def _(src=src, dst=dst):
            pltpu.make_async_copy(src, dst, r_r.at[half_t, par]).start()

        @pl.when(jnp.logical_not(own))
        def _(src=src, dst=dst, dev=dev, g=g):
            pltpu.make_async_remote_copy(
                src_ref=src, dst_ref=dst, send_sem=r_s.at[g], recv_sem=r_r.at[half_t, par],
                device_id=dev, device_id_type=MESH,
            ).start()

    gbuf[t] = jnp.broadcast_to(gain_ref[...].astype(F32), (16, 320)).astype(BF16)
    for d in range(1, 16):
        send(gbuf.at[t], gbuf.at[t], g_s.at[d], g_r.at[d], tdev(d))

    for f in (1, 3, 2):
        near_block(f)

    w_here = yh * 2 + par
    for r, dev in (
        (1, (yh * 16 + mate_z, t)),
        (2, partner),
        (3, ((1 - yh) * 16 + mate_z, t)),
    ):
        send(wo_ref, wob.at[w_here], w_s.at[0, r], w_r.at[0, r], dev)
        rows = pl.ds(pl.multiple_of(w_here * 160, 16), 160)
        send(wm_ref, wmb.at[rows], w_s.at[1, r], w_r.at[1, r], dev)
    wob[w_here] = wo_ref[...]
    wmb[pl.ds(pl.multiple_of(w_here * 160, 16), 160)] = wm_ref[...]

    for d in range(1, 16):
        from_z = lax.rem(z + 16 - d, 16)
        arrived(qrecv.at[pl.ds(from_z * 16, 16)], q_r.at[d])
    lane = iota((STEPS, 256), 1)
    for which in range(2):
        o_y = yh if which == 0 else 1 - yh
        spots = rows_of(STEPS, o_y * 16 + z).astype(I32)
        source = spots >> 7
        diagonal = iota((STEPS, STEPS), 0) == iota((STEPS, STEPS), 1)
        source_row = jnp.sum(
            jnp.where(diagonal, source.astype(F32), 0.0), axis=0, keepdims=True
        ).astype(I32)
        earlier = iota((STEPS, STEPS), 1) < iota((STEPS, STEPS), 0)
        rank = jnp.sum(
            jnp.where((source == source_row) & earlier, 1.0, 0.0), axis=1, keepdims=True
        ).astype(I32)
        for h in range(2):
            wanted = (source & 15) * 16 + o_y * 8 + h * 4 + rank
            take = ((wanted == lane) & (source >> 4 == yh)).astype(BF16)
            rows = nn(take, qrecv[...]).astype(BF16)
            if which == 0:
                qall[h * 160 + TOK : (h + 1) * 160] = rows
            else:
                qmid_s[h * STEPS : (h + 1) * STEPS] = rows
    send(qmid_s, qmid_r, qm_s, qm_r, partner)

    queries = None
    state = [jnp.full((320, 1), MASKED, F32), jnp.zeros((320, 1), F32), jnp.zeros((320, HD), F32)]

    def attend(p, n):
        py = yh if p == 0 else 1 - yh
        set_ = lax.rem(zr + 4 + NEAR[n], 4)
        arrived(kv.at[1 - core, py, set_], c_r.at[p, n])
        keys = kv[0, py, set_].reshape(512, HD)
        values = kv[1, py, set_].reshape(512, HD)
        highest, totals, accum = state
        scores = nt(qall[...], keys) * (HD**-0.5)
        kk = iota((320, 512), 1)
        spot = (py * 16 + set_) * TOK + (kk >> 7) * 512 + (kk & 127)
        scores = jnp.where(spot <= posc[:, 0:1], scores, MASKED)
        new = jnp.maximum(highest, jnp.max(scores, axis=1, keepdims=True))
        alpha = jnp.exp(highest - new)
        weights = jnp.exp(scores - new)
        state[0] = new
        state[1] = totals * alpha + jnp.sum(weights, axis=1, keepdims=True)
        state[2] = accum * alpha + nn(weights.astype(BF16), values)

    waiting = None
    for p in range(2):
        for n in range(4):
            py = yh if p == 0 else 1 - yh
            set_ = lax.rem(zr + 4 + NEAR[n], 4)
            bundle = kv.at[core, py, set_]
            if p == 1:
                arrived(bundle, y_r.at[n])
            elif n > 0:
                for f in range(4):
                    from_z = lax.rem(z + 16 + NEAR[n], 16)
                    arrived(kv.at[core, py, set_, lax.rem(from_z // 4 + 4 - f, 4)], near_r.at[n, f])
            if p == 0:
                send(bundle, bundle, y_s.at[n], y_r.at[n], partner)
            send(bundle, bundle, c_s.at[p, n], c_r.at[p, n], other_core)
            if waiting is None:
                arrived(qmid_r, qm_r)
                for h in range(2):
                    rows = slice(h * 160 + TOK, (h + 1) * 160)
                    qall[rows] = (
                        qall[rows].astype(F32) + qmid_r[h * STEPS : (h + 1) * STEPS].astype(F32)
                    ).astype(BF16)
            else:
                attend(*waiting)
            waiting = (p, n)
    attend(*waiting)
    mixed = (state[2] / state[1]).astype(BF16)
    k_rows = pl.ds(pl.multiple_of(pair * STEPS, STEPS), STEPS)
    for h in range(2):
        agrp[k_rows, h * HD : (h + 1) * HD] = mixed[h * 160 + TOK : (h + 1) * 160]

    for d in (4, 3, 5, 2, 6, 1, 7):
        send(agrp.at[k_rows], agrp.at[k_rows], a_s.at[d], a_r.at[d], zdev(2 * d))
    for h in range(2):
        att_ref[:, h * HD : (h + 1) * HD] = mixed[h * 160 : h * 160 + TOK]

    for r in (1, 2, 3):
        slot = (yh if r < 2 else 1 - yh) * 2 + (par if r % 2 == 0 else 1 - par)
        arrived(wob.at[slot], w_r.at[0, r])
        arrived(wmb.at[pl.ds(pl.multiple_of(slot * 160, 16), 160)], w_r.at[1, r])
    big = nn(wob[0], shift(160, COLS, 0))
    for b in range(1, 4):
        big += nn(wob[b], shift(160, COLS, b * 160))
    wobig[...] = big.astype(BF16)
    wmbig[...] = nn(wmb[...], shift(320, 384, 0)).astype(BF16)
    lwt[...] = jnp.zeros_like(lwt)
    lwt[...] = nn(nt(eye128, lw_ref[...]).astype(BF16), shift(320, 384, 0)).astype(BF16)
    for d in range(1, 16):
        src_t = lax.rem(t + 16 - d, 16)
        arrived(gbuf.at[src_t], g_r.at[d])
    gain = nn(gbuf[pair], shift(320, COLS, 0)) + nn(gbuf[8 + pair], shift(320, COLS, 320))
    gain = gain[0:1]
    for j in range(2):
        for s in range(2):
            arrived(rbuf.at[j, s], r_r.at[j, s])
    row = iota((256, 1), 0)
    spots = rows_of(256, yh * 16 + 2 * (iota((256, 128), 0) >> 5) + par).astype(I32)
    step = (row & 31) * 32 + yh * 16 + 2 * (row >> 5) + par
    slot = iota((256, 64), 1)
    from_second = (spots >> 7) - 2 * t
    rank = jnp.where(from_second == 0, step - before(2 * t * TOK), step - before((2 * t + 1) * TOK)) >> 5
    wanted = jnp.where(
        (from_second == 0) | (from_second == 1), from_second * 32 + (row >> 5) * 4 + rank, 1000
    )
    place = (wanted == slot).astype(BF16)
    res_big = nn(rbuf[0].reshape(64, 320), shift(320, COLS, 0)) + nn(
        rbuf[1].reshape(64, 320), shift(320, COLS, 320)
    )
    res_part = nn(place, res_big.astype(BF16))

    for d in range(1, 8):
        from_k = lax.rem(pair + 8 - d, 8)
        arrived(agrp.at[pl.ds(pl.multiple_of(from_k * STEPS, STEPS), STEPS)], a_r.at[d])
    pb[...] = (nn(agrp[...], wobig[...]) + res_part).astype(BF16)
    for d in range(1, 16):
        to_t = lax.rem(t + d, 16)
        send(pb.at[pl.ds(pl.multiple_of(to_t * 16, 16), 16)], rb.at[t], p_s.at[d], p_r.at[d], tdev(d))
    own_rows = pl.ds(pl.multiple_of(t * 16, 16), 16)
    total = pb[own_rows].astype(F32)
    for d in range(1, 16):
        src_t = lax.rem(t + 16 - d, 16)
        arrived(rb.at[src_t], p_r.at[d])
        total += rb[src_t].astype(F32)
    sb[own_rows] = total.astype(BF16)
    for d in range(1, 16):
        send(sb.at[own_rows], sb.at[own_rows], s_s.at[d], s_r.at[d], tdev(d))
    for d in range(1, 16):
        src_t = lax.rem(t + 16 - d, 16)
        arrived(sb.at[pl.ds(pl.multiple_of(src_t * 16, 16), 16)], s_r.at[d])

    states = sb[...].astype(F32)
    squares = jnp.sum(states * states, axis=1, keepdims=True)
    pre = nn((states * gain).astype(BF16), wmbig[...])
    sq_hi = squares.astype(BF16).astype(F32)
    col = iota((256, 384), 1)
    pre = jnp.where(col == 320, sq_hi, jnp.where(col == 321, squares - sq_hi, pre))
    yb[...] = pre.astype(BF16)
    for d in (4, 3, 5, 2, 6, 1, 7):
        to_k = lax.rem(pair + d, 8)
        send(
            yb.at[pl.ds(pl.multiple_of(to_k * STEPS, STEPS), STEPS)], yr.at[pair], z_s.at[d], z_r.at[d], zdev(2 * d)
        )
    out_k = lax.rem(t, 8)
    block = sb[pl.ds(pl.multiple_of(out_k * STEPS, STEPS), STEPS)]
    ob_s[...] = nn(
        block, (iota((COLS, 320), 0) == iota((COLS, 320), 1) + half_t * 320).astype(BF16)
    ).astype(BF16)
    out_dev = (yh * 16 + 2 * out_k + par, half_t * 8 + pair)
    out_own = (out_dev[0] == c) & (out_dev[1] == t)

    @pl.when(out_own)
    def _():
        pltpu.make_async_copy(ob_s, ob, o_r).start()

    @pl.when(jnp.logical_not(out_own))
    def _():
        pltpu.make_async_remote_copy(
            src_ref=ob_s, dst_ref=ob, send_sem=o_s, recv_sem=o_r, device_id=out_dev, device_id_type=MESH
        ).start()

    total = yb[k_rows].astype(F32)
    for d in range(1, 8):
        from_k = lax.rem(pair + 8 - d, 8)
        arrived(yr.at[from_k], z_r.at[d])
        total += yr[from_k].astype(F32)
    col = iota((STEPS, 384), 1)
    squares = jnp.sum(jnp.where((col == 320) | (col == 321), total, 0.0), axis=1, keepdims=True)
    pre = jnp.where(col < 320, total * lax.rsqrt(squares / D + 1e-06), 0.0)
    hidden = (pre / (1.0 + jnp.exp(-pre))).astype(BF16)
    fb[...] = nt(lwt[...], hidden)
    for d in range(1, 16):
        to_t = lax.rem(t + d, 16)
        send(fb.at[pl.ds(pl.multiple_of(to_t * 8, 8), 8)], fr.at[t], f_s.at[d], f_r.at[d], tdev(d))
    arrived(ob, o_r)
    states_ref[...] = ob[...]
    total = fb[pl.ds(pl.multiple_of(t * 8, 8), 8)]
    for d in range(1, 16):
        src_t = lax.rem(t + 16 - d, 16)
        arrived(fr.at[src_t], f_r.at[d])
        total += fr[src_t]
    levels_ref[...] = total

    for copy in sends:
        copy.wait_send()
    for g in range(4):
        dev = ((g // 2) * 16 + 2 * lax.rem(t, 8) + g % 2, yh * 8 + pair)

        @pl.when(jnp.logical_not((dev[0] == c) & (dev[1] == t)))
        def _(g=g):
            arrived(rsend.at[pl.ds(g * 32, 32)], r_s.at[g])

    @pl.when(jnp.logical_not(out_own))
    def _():
        arrived(ob_s, o_s)


def on_device(q, k, v, res, wo, gain, wm, lw, positions):
    vmem = pl.BlockSpec(memory_space=pltpu.VMEM)
    dma = pltpu.SemaphoreType.DMA
    scratch = [
        pltpu.VMEM((2, 2, 4, 4, TOK, HD), BF16),
        pltpu.VMEM((320, HD), BF16),
        pltpu.VMEM((256, HD), BF16),
        pltpu.VMEM((256, HD), BF16),
        pltpu.VMEM((64, HD), BF16),
        pltpu.VMEM((64, HD), BF16),
        pltpu.VMEM((320, 128), I32),
        pltpu.VMEM((128, 320), BF16),
        pltpu.VMEM((2, 2, 32, 320), BF16),
        pltpu.VMEM((16, 16, 320), BF16),
        pltpu.VMEM((4, 256, 160), BF16),
        pltpu.VMEM((COLS, 320), BF16),
        pltpu.VMEM((256, COLS), BF16),
        pltpu.VMEM((COLS, 384), BF16),
        pltpu.VMEM((128, 384), BF16),
        pltpu.VMEM((256, 256), BF16),
        pltpu.VMEM((256, COLS), BF16),
        pltpu.VMEM((16, 16, COLS), BF16),
        pltpu.VMEM((256, COLS), BF16),
        pltpu.VMEM((32, 320), BF16),
        pltpu.VMEM((32, 320), BF16),
        pltpu.VMEM((256, 384), BF16),
        pltpu.VMEM((8, 32, 384), BF16),
        pltpu.VMEM((128, 32), F32),
        pltpu.VMEM((16, 8, 32), F32),
        dma((4,)), dma((4,)), dma((4, 4)), dma((4, 4)), dma((4,)), dma((4,)), dma((2, 4)), dma((2, 4)),
        dma((16,)), dma((16,)), dma(()), dma(()), dma((4,)), dma((2, 2)), dma((16,)), dma((16,)), dma((2, 4)), dma((2, 4)),
        dma((8,)), dma((8,)), dma((16,)), dma((16,)), dma((16,)), dma((16,)), dma(()), dma(()), dma((8,)), dma((8,)), dma((16,)), dma((16,)),
    ]
    attended, states, levels = pl.pallas_call(
        kernel,
        out_shape=(
            jax.ShapeDtypeStruct((TOK, 2 * HD), BF16),
            jax.ShapeDtypeStruct((STEPS, 320), BF16),
            jax.ShapeDtypeStruct((8, STEPS), F32),
        ),
        in_specs=[vmem] * 9,
        out_specs=(vmem, vmem, vmem),
        scratch_shapes=scratch,
        compiler_params=pltpu.CompilerParams(
            collective_id=0, has_side_effects=True, vmem_limit_bytes=40 * 1024 * 1024
        ),
    )(q, k, v, res, wo, gain.reshape(1, -1), wm, lw, positions.reshape(8, 128))
    return attended, states, levels.T


def solution(mesh):
    in_specs = (
        P("ctx", "tp"),
        P("ctx", None),
        P("ctx", None),
        P("ctx", "tp"),
        P("tp", "ctx"),
        P("tp"),
        P("ctx", "tp"),
        P("tp", None),
        P(),
    )
    out_specs = (P("ctx", "tp"), P("ctx", "tp"), P("ctx", "tp"))
    return jax.shard_map(
        on_device, mesh=mesh, in_specs=in_specs, out_specs=out_specs, check_vma=False
    )
```

time: 747 us -> 111 us (0.15)
  waiting for transfers between devices: 575 us -> 0 us
  blocking collectives: 106 us -> 0 us
  Pallas kernels: 0 us -> 102 us
  between operations: 16 us -> 0.72 us
  starting transfers between devices: 14.9 us -> 0 us
  matrix products: 10.6 us -> 0 us
    all_gather x4 -> x0, waiting for transfers between devices: 501 us -> none  [the longest x1 140 us: on_device(): value_piece = lax.all_gather(value_mine, 'ctx', axis=0, tiled=True)]
    pallas_call x0 -> x1, Pallas kernels: none -> 102 us  [on_device(): pl.pallas_call(kernel, out_shape=(jax.ShapeDtypeStruct((TOK, 2 * HD), BF1...]
    unnamed x1 -> x0, blocking collectives: 56.9 us -> none
    unnamed x6 -> x0, waiting for transfers between devices: 46.5 us -> none
    psum x1 -> x0, blocking collectives: 29.9 us -> none  [on_device(): squares = lax.psum(jnp.sum(states_wide * states_wide, axis=-1), 'tp')]
    all_to_all x2 -> x0, waiting for transfers between devices: 28.1 us -> none  [the longest x1 14.7 us: on_device(): lax.all_to_all(send_attended, 'ctx', split_axis=0, concat_axis=0, tiled=T...]
    all_gather x1 -> x0, blocking collectives: 18.7 us -> none  [on_device(): normed = lax.all_gather(normed_local, 'tp', axis=1, tiled=True)]
    all_to_all x2 -> x0, starting transfers between devices: 14.7 us -> none  [the longest x1 7.44 us: on_device(): lax.all_to_all(send_residual, 'ctx', split_axis=0, concat_axis=0, tiled=T...]
  transfers between devices with their start and end apart: 7 -> 0, of which waited for: 7 -> 0; matrix products, arithmetic and copies ran while one was open for 3% -> 0% of each run, Pallas kernels for 0% -> 0%
where the time goes in v1:
time: 111 us; the launch traced here: 110 us
  Pallas kernels  102 us (92%)
  local copies, waits for them, and re-layouts  7.2 us (6%)
    pallas_call x1, Pallas kernels, on_device(): pl.pallas_call(kernel, out_shape=(jax.ShapeDtypeStruct((TOK, 2 * HD), BF1...  102 us
    unnamed x19, local copies, waits for them, and re-layouts  7.2 us

profile of v1, /device:TPU:1, one launch (start us, length us, event | category | flops | bytes accessed | tf_op | source)
XLA Modules:
  0.0 110.2 jit_solution(11962261559865570821)
XLA Ops:
  0.6 0.0 copy-start.6
  0.6 0.0 copy-start
  0.7 0.7 copy-done.6
  1.3 1.0 copy.12.res_ref
  2.3 0.0 copy-start.2
  2.3 0.0 copy-start.5
  2.3 1.0 copy.13.wo_ref
  3.4 0.0 copy-done
  3.4 0.0 copy-done.2
  3.4 0.0 copy-done.5
  3.4 0.0 copy-start.1
  3.4 0.9 copy-done.1
  4.4 0.0 copy-start.3
  4.4 0.9 copy-done.3
  5.2 0.0 copy-start.4
  5.2 0.8 copy-done.4
  6.1 102.3 %shard_map.112 = (bf16[128,256]{1,0:T(8,128)(2,1)S(1)}, bf16[32,320]{1,0:T(8,128)(2,1)S(1)}, f32[8,32]{1,0:T(8,128)S(1)}) custom-call(bf16[128,256]{1,0:T(8,128)(2,1)S(1)} %copy-done.4, bf16[128,1024]{1,0:T(8,128)(2,1)S(1)} %copy-done, bf16[128,1024]{1,0:T(8,128)(2,1)S(1)} %copy-done.1, bf16[128,320]{1,0:T(8,128)(2,1)S(1)} %copy.12.res_ref, ...), custom_call_target="tpu_custom_call" | custom-call | tf_op jit(solution)/shard_map/pallas_call | solution.py:443
  108.4 0.6 copy.17
  109.0 0.6 copy.18
  109.6 0.6 copy.19
  (1 shorter events, 0.0 us)
Async XLA Ops:
  0.6 0.7 copy-start.6
  0.6 2.7 %copy-start = (bf16[128,1024]{1,0:T(8,128)(2,1)S(1)}, bf16[128,1024]{1,0:T(8,128)(2,1)}, u32[]{:S(2)}) copy-start(bf16[128,1024]{1,0:T(8,128)(2,1)} %k_ref.1) | copy-start | bytes 786436
  2.3 1.1 copy-start.2
  2.3 1.1 copy-start.5
  3.4 1.0 copy-start.1
  4.4 0.9 copy-start.3
  5.2 0.8 copy-start.4

commit v2 on v1

v2 whole, which is shorter than its diff:
```python
import functools

import jax
import jax.numpy as jnp
from jax import lax
from jax.experimental import pallas as pl
from jax.experimental.pallas import tpu as pltpu
from jax.sharding import PartitionSpec as P

D = 5120
HD = 128
TOK = 128
STEPS = 32
COLS = 640
MASKED = -1e30
MESH = pl.DeviceIdType.MESH
F32 = jnp.float32
BF16 = jnp.bfloat16
I32 = jnp.int32


def iota(shape, dim):
    return lax.broadcasted_iota(I32, shape, dim)


def nn(a, b):
    return lax.dot_general(a, b, (((1,), (0,)), ((), ())), preferred_element_type=F32)


def nt(a, b):
    return lax.dot_general(a, b, (((1,), (1,)), ((), ())), preferred_element_type=F32)


def tn(a, b):
    return lax.dot_general(a, b, (((0,), (0,)), ((), ())), preferred_element_type=F32)


def shift(rows, cols, offset):
    return (iota((rows, cols), 0) + offset == iota((rows, cols), 1)).astype(BF16)


def kernel(
    q_hbm, k_hbm, v_hbm, res_hbm, wo_hbm, gain_hbm, wm_hbm, lw_hbm, pos_hbm,
    att_ref, states_ref, levels_ref,
    res_ref, gain_ref, lw_ref, pos_ref, kv, qall, qsend, qrecv, qmid_s, qmid_r, posc,
    rsend, rbuf, gbuf, wob, wmb, wmbig, lwt,
    agrp, res_add, pb, px, ph, rb, sb, ob_s, ob_z, ob, yb, yr, fb, fr,
    in_s, far_s, far_r, near_s, near_r, y_s, y_r, c_s, c_r,
    q_s, q_r, qm_s, qm_r, r_s, r_r, g_s, g_r, w_s, w_r,
    a_s, a_r, x_s, x_r, p_s, p_r, s_s, s_r, o_s, o_r, z_s, z_r, f_s, f_r,
):
    c = lax.axis_index("ctx")
    t = lax.axis_index("tp")
    z = lax.rem(c, 16)
    yh = c // 16
    core = lax.rem(t, 2)
    group = t // 2
    par = lax.rem(z, 2)
    mate_z = z + 1 - 2 * par
    pair = z // 2
    zr = lax.rem(z, 4)
    zq = z // 4
    partner = ((1 - yh) * 16 + z, t)
    other_core = (c, t + 1 - 2 * core)
    sends = []

    def zdev(d):
        return (yh * 16 + lax.rem(z + 16 + d, 16), t)

    def tdev(d):
        return (c, lax.rem(t + d, 16))

    def send(src, dst, ssem, rsem, dev):
        copy = pltpu.make_async_remote_copy(
            src_ref=src, dst_ref=dst, send_sem=ssem, recv_sem=rsem, device_id=dev, device_id_type=MESH
        )
        copy.start()
        sends.append(copy)

    def arrived(dst, rsem):
        pltpu.make_async_copy(dst, dst, rsem).wait()

    barrier = pltpu.get_barrier_semaphore()

    def greet(dev):
        pl.semaphore_signal(barrier, inc=1, device_id=dev, device_id_type=MESH)

    for d in range(1, 16):
        greet(zdev(d))
        greet(tdev(d))
    greet(partner)
    greet(((1 - yh) * 16 + mate_z, t))
    half_t, slot_t = t // 8, lax.rem(t, 8)
    res_to = lax.rem(yh + half_t, 2) * 8 + lax.rem(slot_t + 64 - 3 * pair, 8)
    res_pair = lax.rem(3 * (pair + 8 - slot_t), 8)

    def res_dest(g):
        return ((g // 2) * 16 + 2 * slot_t + g % 2, res_to)

    def res_source(j):
        return lax.rem(half_t + j, 2)

    def elsewhere(dev):
        return jnp.logical_not((dev[0] == c) & (dev[1] == t))

    res_peers = [res_dest(g) for g in range(4)] + [
        (res_source(j) * 16 + 2 * res_pair + p, j * 8 + pair) for j in range(2) for p in range(2)
    ]
    n_peers = 32
    for dev in res_peers:
        n_peers += jnp.where(elsewhere(dev), 1, 0)

        @pl.when(elsewhere(dev))
        def _(dev=dev):
            greet(dev)

    w_here = yh * 2 + par
    wo_rows = pl.ds(pl.multiple_of(w_here * 160, 16), 160)
    lanes = pl.ds(pl.multiple_of(group * HD, HD), HD)
    here = kv.at[core, yh, zr, zq]
    fetches = [
        pltpu.make_async_copy(pos_hbm, pos_ref, in_s.at[0]),
        pltpu.make_async_copy(q_hbm.at[:, pl.ds(0, HD)], qall.at[pl.ds(0, TOK)], in_s.at[1]),
        pltpu.make_async_copy(q_hbm.at[:, pl.ds(HD, HD)], qall.at[pl.ds(160, TOK)], in_s.at[2]),
        pltpu.make_async_copy(res_hbm, res_ref, in_s.at[3]),
        pltpu.make_async_copy(gain_hbm, gain_ref, in_s.at[4]),
        pltpu.make_async_copy(lw_hbm, lw_ref, in_s.at[5]),
        pltpu.make_async_copy(wo_hbm, wob.at[wo_rows], in_s.at[6]),
        pltpu.make_async_copy(wm_hbm, wmb.at[wo_rows], in_s.at[7]),
    ]

    @pl.when(core == 0)
    def _():
        pltpu.make_async_copy(k_hbm.at[:, lanes], here, in_s.at[8]).start()

    @pl.when(core == 1)
    def _():
        pltpu.make_async_copy(v_hbm.at[:, lanes], here, in_s.at[8]).start()

    for fetch in fetches:
        fetch.start()

    fetches[0].wait()
    pos8 = pos_ref[...]
    hi8 = (pos8 >> 6).astype(F32).astype(BF16)
    lo8 = (pos8 & 63).astype(F32).astype(BF16)
    eye128 = shift(128, 128, 0)
    post = (nt(eye128, hi8) * 64.0 + nt(eye128, lo8)).astype(I32)
    base = c * TOK

    def before(limit):
        hits = jnp.where(pos8 < limit, 1.0, 0.0)
        return jnp.sum(jnp.sum(hits, axis=1, keepdims=True), axis=0, keepdims=True).astype(I32)

    first = before(base)
    selq = jnp.zeros((256, TOK), F32)
    selr = jnp.zeros((128, TOK), F32)
    lane_q = iota((128, 256), 1)
    owner_q = ((lane_q >> 3) & 1) * 16 + (lane_q >> 4)
    lane_r = iota((128, 128), 1)
    owner_r = (lane_r >> 6) * 16 + ((lane_r >> 2) & 7) * 2 + ((lane_r >> 5) & 1)
    for a in range(8):
        col = post[:, a : a + 1]
        step = iota((128, 1), 0) + a * 128
        rank = jnp.where((col >= base) & (col < base + TOK), (step - first) >> 5, 1000)
        owner = step & 31
        held = (col == iota((128, TOK), 1) + base).astype(BF16)
        selq += tn(((owner == owner_q) & (rank == (lane_q & 3))).astype(BF16), held)
        selr += tn(((owner == owner_r) & (rank == (lane_r & 3))).astype(BF16), held)
    selq = selq.astype(BF16)
    head_row = (iota((256, 128), 0) >> 2) & 1
    fetches[1].wait()
    fetches[2].wait()
    qsend[...] = jnp.where(
        head_row == 0, nn(selq, qall[0:TOK]), nn(selq, qall[160 : 160 + TOK])
    ).astype(BF16)

    def rows_of(count, owner):
        pick = ((iota((count, 8), 0) & 31) >> 2 == iota((count, 8), 1)).astype(BF16)
        spread = nn(pick, hi8) * 64.0 + nn(pick, lo8)
        lane = (iota((count, 128), 0) & 3) * 32 + owner
        return jnp.sum(jnp.where(iota((count, 128), 1) == lane, spread, 0.0), axis=1, keepdims=True)

    mine = rows_of(STEPS, c)
    for h in range(2):
        posc[h * 160 : h * 160 + TOK] = iota((TOK, 128), 0) + base
        posc[h * 160 + TOK : (h + 1) * 160] = jnp.broadcast_to(mine.astype(I32), (STEPS, 128))

    pl.semaphore_wait(barrier, n_peers)

    arrived(here, in_s.at[8])

    def kv_block(plane, n, f):
        py = yh if plane == 0 else 1 - yh
        from_z = lax.rem(z + (0, 15, 1, 14)[n] + 16 - 4 * f, 16)
        return kv.at[core, py, lax.rem(from_z, 4), from_z // 4]

    def kv_bundle(plane, n, kind):
        py = yh if plane == 0 else 1 - yh
        return kv.at[kind, py, lax.rem(zr + (0, 3, 1, 2)[n], 4)]

    def kv_pass(plane, f):
        block = kv_block(plane, 0, f)
        if plane == 0:
            if f in (0, 1):
                send(block, block, near_s.at[0, 3, f], near_r.at[0, 3, f], zdev(2))
            if f in (0, 3):
                send(block, block, near_s.at[0, 3, 2 + f // 3], near_r.at[0, 3, 2 + f // 3], zdev(-2))
        for n, d in ((1, 1), (2, -1)):
            send(block, block, near_s.at[plane, n, f], near_r.at[plane, n, f], zdev(d))

    def kv_cross(n, f):
        block = kv_block(0, n, f)
        send(block, block, y_s.at[n // 3, f], y_r.at[n // 3, f], partner)

    def kv_core(plane, n):
        bundle = kv_bundle(plane, n, core)
        send(bundle, bundle, c_s.at[plane, n], c_r.at[plane, n], other_core)

    def weight_rows(r):
        slot = (yh if r < 2 else 1 - yh) * 2 + (par if r % 2 == 0 else 1 - par)
        return pl.ds(pl.multiple_of(slot * 160, 16), 160)

    def weight_send(w, r):
        buffer = (wob, wmb)[w]
        rows = weight_rows(1) if r == 3 else wo_rows
        dev = (yh * 16 + mate_z, t) if r == 1 else partner
        send(buffer.at[rows], buffer.at[rows], w_s.at[w, r], w_r.at[w, r], dev)

    def weight_wait(w, r):
        arrived((wob, wmb)[w].at[weight_rows(r)], w_r.at[w, r])

    for f in (2, 1, 3):
        send(here, here, far_s.at[f], far_r.at[f], zdev(4 * f))
    kv_cross(0, 0)
    for d in (8, 7, 9, 6, 10, 5, 11, 4, 12, 3, 13, 2, 14, 1, 15):
        zd = lax.rem(z + d, 16)
        send(
            qsend.at[pl.ds(zd * 16, 16)], qrecv.at[pl.ds(z * 16, 16)], q_s.at[d], q_r.at[d], zdev(d)
        )
    qrecv[pl.ds(pl.multiple_of(z * 16, 16), 16)] = qsend[pl.ds(pl.multiple_of(z * 16, 16), 16)]
    kv_pass(0, 0)
    fetches[6].wait()
    weight_send(0, 2)
    weight_send(0, 1)
    fetches[3].wait()
    rsend[...] = nt(selr.astype(BF16), res_ref[...]).astype(BF16)
    fetches[4].wait()
    gbuf[t] = jnp.broadcast_to(gain_ref[...].astype(F32).reshape(1, 320), (16, 320)).astype(BF16)
    for d in range(1, 16):
        send(gbuf.at[t], gbuf.at[t], g_s.at[d], g_r.at[d], tdev(d))
    fetches[5].wait()
    lwt[...] = nn(nt(eye128, lw_ref[...]).astype(BF16), shift(320, 384, 0)).astype(BF16)

    arrived(kv_block(1, 0, 0), y_r.at[0, 0])
    kv_pass(1, 0)
    for f in (1, 3, 2):
        arrived(kv_block(0, 0, f), far_r.at[f])
        kv_cross(0, f)
        kv_pass(0, f)
    kv_core(0, 0)
    weight_wait(0, 1)
    weight_send(0, 3)

    for d in range(1, 16):
        from_z = lax.rem(z + 16 - d, 16)
        arrived(qrecv.at[pl.ds(from_z * 16, 16)], q_r.at[d])
    lane = iota((STEPS, 256), 1)
    for which in range(2):
        o_y = yh if which == 0 else 1 - yh
        spots = rows_of(STEPS, o_y * 16 + z).astype(I32)
        source = spots >> 7
        diagonal = iota((STEPS, STEPS), 0) == iota((STEPS, STEPS), 1)
        source_row = jnp.sum(
            jnp.where(diagonal, source.astype(F32), 0.0), axis=0, keepdims=True
        ).astype(I32)
        earlier = iota((STEPS, STEPS), 1) < iota((STEPS, STEPS), 0)
        rank = jnp.sum(
            jnp.where((source == source_row) & earlier, 1.0, 0.0), axis=1, keepdims=True
        ).astype(I32)
        for h in range(2):
            wanted = (source & 15) * 16 + o_y * 8 + h * 4 + rank
            take = ((wanted == lane) & (source >> 4 == yh)).astype(BF16)
            rows = nn(take, qrecv[...]).astype(BF16)
            if which == 0:
                qall[h * 160 + TOK : (h + 1) * 160] = rows
            else:
                qmid_s[h * STEPS : (h + 1) * STEPS] = rows
    send(qmid_s, qmid_r, qm_s, qm_r, partner)

    state = [jnp.full((320, 1), MASKED, F32), jnp.zeros((320, 1), F32), jnp.zeros((320, HD), F32)]

    def attend(p, n):
        py = yh if p == 0 else 1 - yh
        set_ = lax.rem(zr + (0, 3, 1, 2)[n], 4)
        arrived(kv_bundle(p, n, 1 - core), c_r.at[p, n])
        keys = kv[0, py, set_].reshape(512, HD)
        values = kv[1, py, set_].reshape(512, HD)
        highest, totals, accum = state
        scores = nt(qall[...], keys) * (HD**-0.5)
        kk = iota((320, 512), 1)
        spot = (py * 16 + set_) * TOK + (kk >> 7) * 512 + (kk & 127)
        scores = jnp.where(spot <= posc[:, 0:1], scores, MASKED)
        new = jnp.maximum(highest, jnp.max(scores, axis=1, keepdims=True))
        alpha = jnp.exp(highest - new)
        weights = jnp.exp(scores - new)
        state[0] = new
        state[1] = totals * alpha + jnp.sum(weights, axis=1, keepdims=True)
        state[2] = accum * alpha + nn(weights.astype(BF16), values)

    for f in (1, 3, 2):
        arrived(kv_block(1, 0, f), y_r.at[0, f])
        kv_pass(1, f)
    kv_core(1, 0)
    arrived(qmid_r, qm_r)
    for h in range(2):
        rows = slice(h * 160 + TOK, (h + 1) * 160)
        qall[rows] = (
            qall[rows].astype(F32) + qmid_r[h * STEPS : (h + 1) * STEPS].astype(F32)
        ).astype(BF16)
    for i, f in ((0, 0), (2, 3), (1, 1), (3, 2)):
        arrived(kv_block(0, 3, f), near_r.at[0, 3, i])
        kv_cross(3, f)
    kv_core(0, 3)
    for g in range(4):
        src = rsend.at[pl.ds(g * 32, 32)]
        dst = rbuf.at[half_t, par]

        @pl.when(jnp.logical_not(elsewhere(res_dest(g))))
        def _(src=src, dst=dst):
            pltpu.make_async_copy(src, dst, r_r.at[half_t, par]).start()

        @pl.when(elsewhere(res_dest(g)))
        def _(src=src, dst=dst, g=g):
            pltpu.make_async_remote_copy(
                src_ref=src, dst_ref=dst, send_sem=r_s.at[g], recv_sem=r_r.at[half_t, par],
                device_id=res_dest(g), device_id_type=MESH,
            ).start()

    attend(0, 0)
    for n in (1, 2):
        for f in range(4):
            arrived(kv_block(0, n, f), near_r.at[0, n, f])
        kv_core(0, n)
    attend(1, 0)
    attend(0, 3)
    for n in (1, 2):
        for f in range(4):
            arrived(kv_block(1, n, f), near_r.at[1, n, f])
        kv_core(1, n)

    for bundle in ((0, 1), (0, 2), (1, 1)):
        attend(*bundle)
    for f in range(4):
        arrived(kv_block(1, 3, f), y_r.at[1, f])
    kv_core(1, 3)
    attend(1, 2)
    attend(1, 3)
    mixed = (state[2] / state[1]).astype(BF16)
    k_rows = pl.ds(pl.multiple_of(pair * STEPS, STEPS), STEPS)
    for h in range(2):
        agrp[k_rows, h * HD : (h + 1) * HD] = mixed[h * 160 + TOK : (h + 1) * 160]

    for d in (4, 3, 5, 2, 6, 1, 7):
        send(agrp.at[k_rows], agrp.at[k_rows], a_s.at[d], a_r.at[d], zdev(2 * d))
    for h in range(2):
        att_ref[:, h * HD : (h + 1) * HD] = mixed[h * 160 : h * 160 + TOK]

    for d in range(1, 16):
        src_t = lax.rem(t + 16 - d, 16)
        arrived(gbuf.at[src_t], g_r.at[d])
    gain = nn(gbuf[pair], shift(320, COLS, 0)) + nn(gbuf[8 + pair], shift(320, COLS, 320))
    gain = gain[0:1]
    for j in range(2):
        for s in range(2):
            arrived(rbuf.at[j, s], r_r.at[j, s])
    row = iota((256, 1), 0)
    spots = rows_of(256, yh * 16 + 2 * (iota((256, 128), 0) >> 5) + par).astype(I32)
    step = (row & 31) * 32 + yh * 16 + 2 * (row >> 5) + par
    slot = iota((256, 64), 1)
    res_part = jnp.zeros((256, COLS), F32)
    for j in range(2):
        source = res_source(j) * 16 + 2 * res_pair
        nth = (spots >> 7) - source
        rank = (step - jnp.where(nth == 0, before(source * TOK), before((source + 1) * TOK))) >> 5
        wanted = jnp.where((nth == 0) | (nth == 1), nth * 32 + (row >> 5) * 4 + rank, 1000)
        rows = nn((wanted == slot).astype(BF16), rbuf[j].reshape(64, 320)).astype(BF16)
        res_part += nn(rows, shift(320, COLS, j * 320))

    res_add[...] = res_part

    weight_wait(0, 2)
    weight_wait(0, 3)
    for d in range(1, 8):
        from_k = lax.rem(pair + 8 - d, 8)
        arrived(agrp.at[pl.ds(pl.multiple_of(from_k * STEPS, STEPS), STEPS)], a_r.at[d])
    mine = pl.ds(pl.multiple_of(core * 128, 128), 128)
    theirs = pl.ds(pl.multiple_of((1 - core) * 128, 128), 128)
    chip = t // 2
    pb[...] = (nt(agrp[theirs], wob[...]) + res_add[theirs]).astype(BF16)
    send(pb, px, x_s.at[0], x_r.at[0], other_core)
    partial = nt(agrp[mine], wob[...]) + res_add[mine]
    arrived(px, x_r.at[0])
    ph[...] = (partial + px[...].astype(F32)).astype(BF16)

    def chip_rows(index):
        return pl.ds(pl.multiple_of(index * 16, 16), 16)

    for d in (4, 3, 5, 2, 6, 1, 7):
        send(ph.at[chip_rows(lax.rem(chip + d, 8))], rb.at[chip], p_s.at[d], p_r.at[d], tdev(2 * d))
    fetches[7].wait()
    weight_send(1, 1)
    weight_send(1, 2)
    total = ph[chip_rows(chip)].astype(F32)
    for d in range(1, 8):
        src = lax.rem(chip + 8 - d, 8)
        arrived(rb.at[src], p_r.at[d])
        total += rb[src].astype(F32)
    own_rows = chip_rows(core * 8 + chip)
    sb[own_rows] = total.astype(BF16)
    for d in (4, 3, 5, 2, 6, 1, 7):
        send(sb.at[own_rows], sb.at[own_rows], s_s.at[d], s_r.at[d], tdev(2 * d))
    weight_wait(1, 1)
    weight_send(1, 3)
    weight_wait(1, 2)
    for d in range(1, 8):
        arrived(sb.at[chip_rows(core * 8 + lax.rem(chip + 8 - d, 8))], s_r.at[d])
    send(sb.at[mine], sb.at[mine], x_s.at[1], x_r.at[1], other_core)
    weight_wait(1, 3)
    wmbig[...] = nn(wmb[...], shift(320, 384, 0)).astype(BF16)

    def score(rows, first_owner):
        states = sb[rows].astype(F32)
        squares = jnp.sum(states * states, axis=1, keepdims=True)
        pre = nn((states * gain).astype(BF16), wmbig[...])
        sq_hi = squares.astype(BF16).astype(F32)
        col = iota((128, 384), 1)
        pre = jnp.where(col == 320, sq_hi, jnp.where(col == 321, squares - sq_hi, pre))
        yb[rows] = pre.astype(BF16)
        for m in range(4):
            k = first_owner + m
            piece = yb.at[pl.ds(pl.multiple_of(k * STEPS, STEPS), STEPS)]

            @pl.when(k != pair)
            def _(k=k, piece=piece):
                pltpu.make_async_remote_copy(
                    src_ref=piece, dst_ref=yr.at[pair], send_sem=z_s.at[k], recv_sem=z_r.at[pair],
                    device_id=(yh * 16 + 2 * k + par, t), device_id_type=MESH,
                ).start()

    score(mine, core * 4)
    arrived(sb.at[theirs], x_r.at[1])
    score(theirs, (1 - core) * 4)

    out_k = lax.rem(slot_t + 3 * pair, 8)
    block = sb[pl.ds(pl.multiple_of(out_k * STEPS, STEPS), STEPS)]
    ob_s[...] = nn(
        block, (iota((COLS, 320), 0) == iota((COLS, 320), 1) + half_t * 320).astype(BF16)
    ).astype(BF16)

    def out_send(src, dst, n, dev):
        @pl.when(elsewhere(dev))
        def _():
            pltpu.make_async_remote_copy(
                src_ref=src, dst_ref=dst, send_sem=o_s.at[n], recv_sem=o_r.at[n], device_id=dev, device_id_type=MESH
            ).start()

        @pl.when(jnp.logical_not(elsewhere(dev)))
        def _():
            pltpu.make_async_copy(src, dst, o_r.at[n]).start()

    out_z = (yh * 16 + 2 * out_k + par, t)
    out_t = (c, half_t * 8 + lax.rem(3 * (pair + 8 - slot_t), 8))
    out_send(ob_s, ob_z, 0, out_z)

    yr[pair] = yb[k_rows]
    for k in range(8):

        @pl.when(k != pair)
        def _(k=k):
            arrived(yr.at[k], z_r.at[k])

    total = yr[0].astype(F32)
    for k in range(1, 8):
        total += yr[k].astype(F32)
    col = iota((STEPS, 384), 1)
    squares = jnp.sum(jnp.where((col == 320) | (col == 321), total, 0.0), axis=1, keepdims=True)
    pre = jnp.where(col < 320, total * lax.rsqrt(squares / D + 1e-06), 0.0)
    arrived(ob_z, o_r.at[0])
    out_send(ob_z, ob, 1, out_t)
    hidden = (pre / (1.0 + jnp.exp(-pre))).astype(BF16)
    fb[...] = nt(lwt[...], hidden)
    for d in range(1, 16):
        to_t = lax.rem(t + d, 16)
        send(fb.at[pl.ds(pl.multiple_of(to_t * 8, 8), 8)], fr.at[t], f_s.at[d], f_r.at[d], tdev(d))
    arrived(ob, o_r.at[1])
    states_ref[...] = ob[...]
    total = fb[pl.ds(pl.multiple_of(t * 8, 8), 8)]
    for d in range(1, 16):
        src_t = lax.rem(t + 16 - d, 16)
        arrived(fr.at[src_t], f_r.at[d])
        total += fr[src_t]
    levels_ref[...] = total

    for copy in sends:
        copy.wait_send()
    for g in range(4):

        @pl.when(elsewhere(res_dest(g)))
        def _(g=g):
            arrived(rsend.at[pl.ds(g * 32, 32)], r_s.at[g])

    for k in range(8):

        @pl.when(k != pair)
        def _(k=k):
            arrived(yr.at[k], z_s.at[k])

    for n, dev in enumerate((out_z, out_t)):

        @pl.when(elsewhere(dev))
        def _(n=n):
            arrived(ob, o_s.at[n])


def on_device(q, k, v, res, wo, gain, wm, lw, positions):
    vmem = pl.BlockSpec(memory_space=pltpu.VMEM)
    dma = pltpu.SemaphoreType.DMA
    scratch = [
        pltpu.VMEM((320, TOK), BF16),
        pltpu.VMEM((320,), BF16),
        pltpu.VMEM((320, 128), BF16),
        pltpu.VMEM((8, 128), I32),
        pltpu.VMEM((2, 2, 4, 4, TOK, HD), BF16),
        pltpu.VMEM((320, HD), BF16),
        pltpu.VMEM((256, HD), BF16),
        pltpu.VMEM((256, HD), BF16),
        pltpu.VMEM((64, HD), BF16),
        pltpu.VMEM((64, HD), BF16),
        pltpu.VMEM((320, 128), I32),
        pltpu.VMEM((128, 320), BF16),
        pltpu.VMEM((2, 2, 32, 320), BF16),
        pltpu.VMEM((16, 16, 320), BF16),
        pltpu.VMEM((COLS, 256), BF16),
        pltpu.VMEM((COLS, 320), BF16),
        pltpu.VMEM((COLS, 384), BF16),
        pltpu.VMEM((128, 384), BF16),
        pltpu.VMEM((256, 256), BF16),
        pltpu.VMEM((256, COLS), F32),
        pltpu.VMEM((128, COLS), BF16),
        pltpu.VMEM((128, COLS), BF16),
        pltpu.VMEM((128, COLS), BF16),
        pltpu.VMEM((8, 16, COLS), BF16),
        pltpu.VMEM((256, COLS), BF16),
        pltpu.VMEM((32, 320), BF16),
        pltpu.VMEM((32, 320), BF16),
        pltpu.VMEM((32, 320), BF16),
        pltpu.VMEM((256, 384), BF16),
        pltpu.VMEM((8, 32, 384), BF16),
        pltpu.VMEM((128, 32), F32),
        pltpu.VMEM((16, 8, 32), F32),
        dma((9,)), dma((4,)), dma((4,)), dma((2, 4, 4)), dma((2, 4, 4)), dma((2, 4)), dma((2, 4)), dma((2, 4)), dma((2, 4)),
        dma((16,)), dma((16,)), dma(()), dma(()), dma((4,)), dma((2, 2)), dma((16,)), dma((16,)), dma((2, 4)), dma((2, 4)),
        dma((8,)), dma((8,)), dma((2,)), dma((2,)), dma((8,)), dma((8,)), dma((8,)), dma((8,)), dma((2,)), dma((2,)), dma((8,)), dma((8,)), dma((16,)), dma((16,)),
    ]
    attended, states, levels = pl.pallas_call(
        kernel,
        out_shape=(
            jax.ShapeDtypeStruct((TOK, 2 * HD), BF16),
            jax.ShapeDtypeStruct((STEPS, 320), BF16),
            jax.ShapeDtypeStruct((8, STEPS), F32),
        ),
        in_specs=[pl.BlockSpec(memory_space=pltpu.HBM)] * 9,
        out_specs=(vmem, vmem, vmem),
        scratch_shapes=scratch,
        compiler_params=pltpu.CompilerParams(
            collective_id=0, has_side_effects=True, vmem_limit_bytes=56 * 1024 * 1024
        ),
    )(q, k, v, res.T, wo.T, gain, wm, lw, positions.reshape(8, 128))
    return attended, states, levels.T


def solution(mesh):
    in_specs = (
        P("ctx", "tp"),
        P("ctx", None),
        P("ctx", None),
        P("ctx", "tp"),
        P("tp", "ctx"),
        P("tp"),
        P("ctx", "tp"),
        P("tp", None),
        P(),
    )
    out_specs = (P("ctx", "tp"), P("ctx", "tp"), P("ctx", "tp"))
    return jax.shard_map(
        on_device, mesh=mesh, in_specs=in_specs, out_specs=out_specs, check_vma=False
    )
```

time: 111 us -> 97 us (0.87)
  Pallas kernels: 102 us -> 92.5 us
  local copies, waits for them, and re-layouts: 7.2 us -> 2.76 us
    pallas_call x1, Pallas kernels: 102 us -> 92.5 us  [on_device(): pl.pallas_call(kernel, out_shape=(jax.ShapeDtypeStruct((TOK, 2 * HD), BF1...]
    unnamed x19 -> x7, local copies, waits for them, and re-layouts: 7.2 us -> 2.76 us
where the time goes in v2:
time: 97 us; the launch traced here: 95.9 us
  Pallas kernels  92.5 us (95%)
  local copies, waits for them, and re-layouts  2.76 us (3%)
    pallas_call x1, Pallas kernels, on_device(): pl.pallas_call(kernel, out_shape=(jax.ShapeDtypeStruct((TOK, 2 * HD), BF1...  92.5 us
    unnamed x7, local copies, waits for them, and re-layouts  2.76 us

profile of v2, /device:TPU:1, one launch (start us, length us, event | category | flops | bytes accessed | tf_op | source)
XLA Modules:
  0.0 95.9 jit_solution(14726623764770346723)
XLA Ops:
  0.6 92.5 %shard_map.112 = (bf16[128,256]{1,0:T(8,128)(2,1)}, bf16[32,320]{1,0:T(8,128)(2,1)}, f32[8,32]{1,0:T(8,128)}) custom-call(bf16[128,256]{1,0:T(8,128)(2,1)} %q_hbm.1, bf16[128,1024]{1,0:T(8,128)(2,1)} %k_hbm.1, bf16[128,1024]{1,0:T(8,128)(2,1)} %v_hbm.1, bf16[320,128]{1,0:T(8,128)(2,1)} %bitcast.4, bf16[160,256]{1,0:T(8,128)(2,1)} %bitcast.5, ...), custom_call_target="tpu_custom_call" | custom-call | tf_op jit(solution)/shard_map/pallas_call | solution.py:566
  93.2 0.0 copy-start
  93.2 1.5 %copy.15 = bf16[128,256]{1,0:T(8,128)(2,1)} copy(bf16[128,256]{1,0:T(8,128)(2,1)} %get-tuple-element.12) | data formatting | bytes 131072
  94.6 0.0 copy-done
  94.6 0.0 copy-start.1
  94.6 0.6 copy.16
  95.3 0.1 copy-done.1
  95.3 0.6 copy.17
Async XLA Ops:
  93.2 1.5 %copy-start = (bf16[32,320]{1,0:T(8,128)(2,1)S(1)}, bf16[32,320]{1,0:T(8,128)(2,1)}, u32[]{:S(2)}) copy-start(bf16[32,320]{1,0:T(8,128)(2,1)} %get-tuple-element.13) | copy-start | bytes 61444
  94.6 0.7 copy-start.1

commit v3 on v2

--- a/solution.py
+++ b/solution.py
@@ -43,10 +43,10 @@
     q_hbm, k_hbm, v_hbm, res_hbm, wo_hbm, gain_hbm, wm_hbm, lw_hbm, pos_hbm,
     att_ref, states_ref, levels_ref,
     res_ref, gain_ref, lw_ref, pos_ref, kv, qall, qsend, qrecv, qmid_s, qmid_r, posc,
-    rsend, rbuf, gbuf, wob, wmb, wmbig, lwt,
+    rsend, rmid, rbuf, gbuf, wob, wmb, wmbig, lwt,
     agrp, res_add, pb, px, ph, rb, sb, ob_s, ob_z, ob, yb, yr, fb, fr,
     in_s, far_s, far_r, near_s, near_r, y_s, y_r, c_s, c_r,
-    q_s, q_r, qm_s, qm_r, r_s, r_r, g_s, g_r, w_s, w_r,
+    q_s, q_r, qm_s, qm_r, m_s, m_r, r_s, r_r, g_s, g_r, w_s, w_r,
     a_s, a_r, x_s, x_r, p_s, p_r, s_s, s_r, o_s, o_r, z_s, z_r, f_s, f_r,
 ):
     c = lax.axis_index("ctx")
@@ -77,6 +77,25 @@
         copy.start()
         sends.append(copy)
 
+    def elsewhere(dev):
+        return jnp.logical_not((dev[0] == c) & (dev[1] == t))
+
+    def either(src, dst, ssem, rsem, dev):
+        @pl.when(elsewhere(dev))
+        def _():
+            pltpu.make_async_remote_copy(
+                src_ref=src, dst_ref=dst, send_sem=ssem, recv_sem=rsem, device_id=dev, device_id_type=MESH
+            ).start()
+
+        @pl.when(jnp.logical_not(elsewhere(dev)))
+        def _():
+            pltpu.make_async_copy(src, dst, rsem).start()
+
+    def either_sent(src, ssem, dev):
+        @pl.when(elsewhere(dev))
+        def _():
+            arrived(src, ssem)
+
     def arrived(dst, rsem):
         pltpu.make_async_copy(dst, dst, rsem).wait()
 
@@ -91,20 +110,19 @@
     greet(partner)
     greet(((1 - yh) * 16 + mate_z, t))
     half_t, slot_t = t // 8, lax.rem(t, 8)
-    res_to = lax.rem(yh + half_t, 2) * 8 + lax.rem(slot_t + 64 - 3 * pair, 8)
+    res_mid = (c, lax.rem(yh + half_t, 2) * 8 + lax.rem(slot_t + 64 - 3 * pair, 8))
+    held_pair = lax.rem(slot_t + 3 * pair, 8)
+    held_half = lax.rem(half_t + yh, 2)
     res_pair = lax.rem(3 * (pair + 8 - slot_t), 8)
 
     def res_dest(g):
-        return ((g // 2) * 16 + 2 * slot_t + g % 2, res_to)
+        return ((g // 2) * 16 + 2 * held_pair + g % 2, t)
 
     def res_source(j):
         return lax.rem(half_t + j, 2)
 
-    def elsewhere(dev):
-        return jnp.logical_not((dev[0] == c) & (dev[1] == t))
-
     res_peers = [res_dest(g) for g in range(4)] + [
-        (res_source(j) * 16 + 2 * res_pair + p, j * 8 + pair) for j in range(2) for p in range(2)
+        (res_source(j) * 16 + 2 * res_pair + p, t) for j in range(2) for p in range(2)
     ]
     n_peers = 32
     for dev in res_peers:
@@ -154,19 +172,18 @@
 
     first = before(base)
     selq = jnp.zeros((256, TOK), F32)
-    selr = jnp.zeros((128, TOK), F32)
     lane_q = iota((128, 256), 1)
     owner_q = ((lane_q >> 3) & 1) * 16 + (lane_q >> 4)
-    lane_r = iota((128, 128), 1)
-    owner_r = (lane_r >> 6) * 16 + ((lane_r >> 2) & 7) * 2 + ((lane_r >> 5) & 1)
-    for a in range(8):
+
+    def held_steps(a):
         col = post[:, a : a + 1]
         step = iota((128, 1), 0) + a * 128
         rank = jnp.where((col >= base) & (col < base + TOK), (step - first) >> 5, 1000)
-        owner = step & 31
-        held = (col == iota((128, TOK), 1) + base).astype(BF16)
+        return step & 31, rank, (col == iota((128, TOK), 1) + base).astype(BF16)
+
+    for a in range(8):
+        owner, rank, held = held_steps(a)
         selq += tn(((owner == owner_q) & (rank == (lane_q & 3))).astype(BF16), held)
-        selr += tn(((owner == owner_r) & (rank == (lane_r & 3))).astype(BF16), held)
     selq = selq.astype(BF16)
     head_row = (iota((256, 128), 0) >> 2) & 1
     fetches[1].wait()
@@ -180,11 +197,6 @@
         spread = nn(pick, hi8) * 64.0 + nn(pick, lo8)
         lane = (iota((count, 128), 0) & 3) * 32 + owner
         return jnp.sum(jnp.where(iota((count, 128), 1) == lane, spread, 0.0), axis=1, keepdims=True)
-
-    mine = rows_of(STEPS, c)
-    for h in range(2):
-        posc[h * 160 : h * 160 + TOK] = iota((TOK, 128), 0) + base
-        posc[h * 160 + TOK : (h + 1) * 160] = jnp.broadcast_to(mine.astype(I32), (STEPS, 128))
 
     pl.semaphore_wait(barrier, n_peers)
 
@@ -243,9 +255,20 @@
     fetches[6].wait()
     weight_send(0, 2)
     weight_send(0, 1)
+    mine = rows_of(STEPS, c)
+    for h in range(2):
+        posc[h * 160 : h * 160 + TOK] = iota((TOK, 128), 0) + base
+        posc[h * 160 + TOK : (h + 1) * 160] = jnp.broadcast_to(mine.astype(I32), (STEPS, 128))
+    selr = jnp.zeros((128, TOK), F32)
+    lane_r = iota((128, 128), 1)
+    owner_r = (lane_r >> 6) * 16 + ((lane_r >> 2) & 7) * 2 + ((lane_r >> 5) & 1)
+    for a in range(8):
+        owner, rank, held = held_steps(a)
+        selr += tn(((owner == owner_r) & (rank == (lane_r & 3))).astype(BF16), held)
     fetches[3].wait()
     rsend[...] = nt(selr.astype(BF16), res_ref[...]).astype(BF16)
     fetches[4].wait()
+    either(rsend, rmid, m_s, m_r, res_mid)
     gbuf[t] = jnp.broadcast_to(gain_ref[...].astype(F32).reshape(1, 320), (16, 320)).astype(BF16)
     for d in range(1, 16):
         send(gbuf.at[t], gbuf.at[t], g_s.at[d], g_r.at[d], tdev(d))
@@ -254,10 +277,25 @@
 
     arrived(kv_block(1, 0, 0), y_r.at[0, 0])
     kv_pass(1, 0)
-    for f in (1, 3, 2):
+
+    def kv_far(f):
         arrived(kv_block(0, 0, f), far_r.at[f])
         kv_cross(0, f)
         kv_pass(0, f)
+
+    def kv_two(i, f):
+        arrived(kv_block(0, 3, f), near_r.at[0, 3, i])
+        kv_cross(3, f)
+
+    def kv_other(f):
+        arrived(kv_block(1, 0, f), y_r.at[0, f])
+        kv_pass(1, f)
+
+    kv_far(1)
+    kv_far(3)
+    kv_two(0, 0)
+    kv_two(2, 3)
+    kv_far(2)
     kv_core(0, 0)
     weight_wait(0, 1)
     weight_send(0, 3)
@@ -308,9 +346,12 @@
         state[1] = totals * alpha + jnp.sum(weights, axis=1, keepdims=True)
         state[2] = accum * alpha + nn(weights.astype(BF16), values)
 
-    for f in (1, 3, 2):
-        arrived(kv_block(1, 0, f), y_r.at[0, f])
-        kv_pass(1, f)
+    kv_other(1)
+    kv_other(3)
+    kv_two(1, 1)
+    kv_two(3, 2)
+    kv_core(0, 3)
+    kv_other(2)
     kv_core(1, 0)
     arrived(qmid_r, qm_r)
     for h in range(2):
@@ -318,24 +359,9 @@
         qall[rows] = (
             qall[rows].astype(F32) + qmid_r[h * STEPS : (h + 1) * STEPS].astype(F32)
         ).astype(BF16)
-    for i, f in ((0, 0), (2, 3), (1, 1), (3, 2)):
-        arrived(kv_block(0, 3, f), near_r.at[0, 3, i])
-        kv_cross(3, f)
-    kv_core(0, 3)
+    arrived(rmid, m_r)
     for g in range(4):
-        src = rsend.at[pl.ds(g * 32, 32)]
-        dst = rbuf.at[half_t, par]
-
-        @pl.when(jnp.logical_not(elsewhere(res_dest(g))))
-        def _(src=src, dst=dst):
-            pltpu.make_async_copy(src, dst, r_r.at[half_t, par]).start()
-
-        @pl.when(elsewhere(res_dest(g)))
-        def _(src=src, dst=dst, g=g):
-            pltpu.make_async_remote_copy(
-                src_ref=src, dst_ref=dst, send_sem=r_s.at[g], recv_sem=r_r.at[half_t, par],
-                device_id=res_dest(g), device_id_type=MESH,
-            ).start()
+        either(rmid.at[pl.ds(g * 32, 32)], rbuf.at[held_half, par], r_s.at[g], r_r.at[held_half, par], res_dest(g))
 
     attend(0, 0)
     for n in (1, 2):
@@ -458,20 +484,9 @@
         block, (iota((COLS, 320), 0) == iota((COLS, 320), 1) + half_t * 320).astype(BF16)
     ).astype(BF16)
 
-    def out_send(src, dst, n, dev):
-        @pl.when(elsewhere(dev))
-        def _():
-            pltpu.make_async_remote_copy(
-                src_ref=src, dst_ref=dst, send_sem=o_s.at[n], recv_sem=o_r.at[n], device_id=dev, device_id_type=MESH
-            ).start()
-
-        @pl.when(jnp.logical_not(elsewhere(dev)))
-        def _():
-            pltpu.make_async_copy(src, dst, o_r.at[n]).start()
-
     out_z = (yh * 16 + 2 * out_k + par, t)
     out_t = (c, half_t * 8 + lax.rem(3 * (pair + 8 - slot_t), 8))
-    out_send(ob_s, ob_z, 0, out_z)
+    either(ob_s, ob_z, o_s.at[0], o_r.at[0], out_z)
 
     yr[pair] = yb[k_rows]
     for k in range(8):
@@ -487,7 +502,7 @@
     squares = jnp.sum(jnp.where((col == 320) | (col == 321), total, 0.0), axis=1, keepdims=True)
     pre = jnp.where(col < 320, total * lax.rsqrt(squares / D + 1e-06), 0.0)
     arrived(ob_z, o_r.at[0])
-    out_send(ob_z, ob, 1, out_t)
+    either(ob_z, ob, o_s.at[1], o_r.at[1], out_t)
     hidden = (pre / (1.0 + jnp.exp(-pre))).astype(BF16)
     fb[...] = nt(lwt[...], hidden)
     for d in range(1, 16):
@@ -504,11 +519,9 @@
 
     for copy in sends:
         copy.wait_send()
+    either_sent(rsend, m_s, res_mid)
     for g in range(4):
-
-        @pl.when(elsewhere(res_dest(g)))
-        def _(g=g):
-            arrived(rsend.at[pl.ds(g * 32, 32)], r_s.at[g])
+        either_sent(rmid.at[pl.ds(g * 32, 32)], r_s.at[g], res_dest(g))
 
     for k in range(8):
 
@@ -516,11 +529,8 @@
         def _(k=k):
             arrived(yr.at[k], z_s.at[k])
 
-    for n, dev in enumerate((out_z, out_t)):
-
-        @pl.when(elsewhere(dev))
-        def _(n=n):
-            arrived(ob, o_s.at[n])
+    either_sent(ob_s, o_s.at[0], out_z)
+    either_sent(ob_z, o_s.at[1], out_t)
 
 
 def on_device(q, k, v, res, wo, gain, wm, lw, positions):
@@ -538,6 +548,7 @@
         pltpu.VMEM((64, HD), BF16),
         pltpu.VMEM((64, HD), BF16),
         pltpu.VMEM((320, 128), I32),
+        pltpu.VMEM((128, 320), BF16),
         pltpu.VMEM((128, 320), BF16),
         pltpu.VMEM((2, 2, 32, 320), BF16),
         pltpu.VMEM((16, 16, 320), BF16),
@@ -560,7 +571,7 @@
         pltpu.VMEM((128, 32), F32),
         pltpu.VMEM((16, 8, 32), F32),
         dma((9,)), dma((4,)), dma((4,)), dma((2, 4, 4)), dma((2, 4, 4)), dma((2, 4)), dma((2, 4)), dma((2, 4)), dma((2, 4)),
-        dma((16,)), dma((16,)), dma(()), dma(()), dma((4,)), dma((2, 2)), dma((16,)), dma((16,)), dma((2, 4)), dma((2, 4)),
+        dma((16,)), dma((16,)), dma(()), dma(()), dma(()), dma(()), dma((4,)), dma((2, 2)), dma((16,)), dma((16,)), dma((2, 4)), dma((2, 4)),
         dma((8,)), dma((8,)), dma((2,)), dma((2,)), dma((8,)), dma((8,)), dma((8,)), dma((8,)), dma((2,)), dma((2,)), dma((8,)), dma((8,)), dma((16,)), dma((16,)),
     ]
     attended, states, levels = pl.pallas_call(

time: 97 us -> 91.8 us (0.946)
  Pallas kernels: 92.5 us -> 88.2 us
    pallas_call x1, Pallas kernels: 92.5 us -> 88.2 us  [on_device(): pl.pallas_call(kernel, out_shape=(jax.ShapeDtypeStruct((TOK, 2 * HD), BF1...]
where the time goes in v3:
time: 91.8 us; the launch traced here: 91.6 us
  Pallas kernels  88.2 us (96%)
  local copies, waits for them, and re-layouts  2.76 us (3%)
    pallas_call x1, Pallas kernels, on_device(): pl.pallas_call(kernel, out_shape=(jax.ShapeDtypeStruct((TOK, 2 * HD), BF1...  88.2 us
    unnamed x7, local copies, waits for them, and re-layouts  2.76 us

profile of v3, /device:TPU:1, one launch (start us, length us, event | category | flops | bytes accessed | tf_op | source)
XLA Modules:
  0.0 91.6 jit_solution(4073680968708394588)
XLA Ops:
  0.6 88.2 %shard_map.112 = (bf16[128,256]{1,0:T(8,128)(2,1)}, bf16[32,320]{1,0:T(8,128)(2,1)}, f32[8,32]{1,0:T(8,128)}) custom-call(bf16[128,256]{1,0:T(8,128)(2,1)} %q_hbm.1, bf16[128,1024]{1,0:T(8,128)(2,1)} %k_hbm.1, bf16[128,1024]{1,0:T(8,128)(2,1)} %v_hbm.1, bf16[320,128]{1,0:T(8,128)(2,1)} %bitcast.4, bf16[160,256]{1,0:T(8,128)(2,1)} %bitcast.5, ...), custom_call_target="tpu_custom_call" | custom-call | tf_op jit(solution)/shard_map/pallas_call | solution.py:577
  88.8 0.0 copy-start
  88.9 1.5 %copy.15 = bf16[128,256]{1,0:T(8,128)(2,1)} copy(bf16[128,256]{1,0:T(8,128)(2,1)} %get-tuple-element.12) | data formatting | bytes 131072
  90.3 0.0 copy-done
  90.3 0.0 copy-start.1
  90.3 0.6 copy.16
  91.0 0.1 copy-done.1
  91.0 0.6 copy.17
Async XLA Ops:
  88.8 1.5 %copy-start = (bf16[32,320]{1,0:T(8,128)(2,1)S(1)}, bf16[32,320]{1,0:T(8,128)(2,1)}, u32[]{:S(2)}) copy-start(bf16[32,320]{1,0:T(8,128)(2,1)} %get-tuple-element.13) | copy-start | bytes 61444
  90.3 0.7 copy-start.1

commit v4 on v3

--- a/solution.py
+++ b/solution.py
@@ -163,7 +163,6 @@
     hi8 = (pos8 >> 6).astype(F32).astype(BF16)
     lo8 = (pos8 & 63).astype(F32).astype(BF16)
     eye128 = shift(128, 128, 0)
-    post = (nt(eye128, hi8) * 64.0 + nt(eye128, lo8)).astype(I32)
     base = c * TOK
 
     def before(limit):
@@ -172,18 +171,19 @@
 
     first = before(base)
     selq = jnp.zeros((256, TOK), F32)
-    lane_q = iota((128, 256), 1)
-    owner_q = ((lane_q >> 3) & 1) * 16 + (lane_q >> 4)
+    slot_q = iota((256, 128), 0)
+    key_q = (((slot_q >> 3) & 1) * 16 + (slot_q >> 4)) * 4 + (slot_q & 3)
 
     def held_steps(a):
-        col = post[:, a : a + 1]
-        step = iota((128, 1), 0) + a * 128
-        rank = jnp.where((col >= base) & (col < base + TOK), (step - first) >> 5, 1000)
-        return step & 31, rank, (col == iota((128, TOK), 1) + base).astype(BF16)
+        spot = pos8[a : a + 1]
+        step = iota((1, 128), 1) + a * 128
+        here_too = (spot >= base) & (spot < base + TOK)
+        key = jnp.where(here_too, (step & 31) * 4 + ((step - first) >> 5), -1)
+        return key, (spot == iota((TOK, 128), 0) + base).astype(BF16)
 
     for a in range(8):
-        owner, rank, held = held_steps(a)
-        selq += tn(((owner == owner_q) & (rank == (lane_q & 3))).astype(BF16), held)
+        key, held = held_steps(a)
+        selq += nt((key == key_q).astype(BF16), held)
     selq = selq.astype(BF16)
     head_row = (iota((256, 128), 0) >> 2) & 1
     fetches[1].wait()
@@ -254,17 +254,19 @@
     kv_pass(0, 0)
     fetches[6].wait()
     weight_send(0, 2)
+    fetches[7].wait()
+    weight_send(1, 2)
     weight_send(0, 1)
     mine = rows_of(STEPS, c)
     for h in range(2):
         posc[h * 160 : h * 160 + TOK] = iota((TOK, 128), 0) + base
         posc[h * 160 + TOK : (h + 1) * 160] = jnp.broadcast_to(mine.astype(I32), (STEPS, 128))
     selr = jnp.zeros((128, TOK), F32)
-    lane_r = iota((128, 128), 1)
-    owner_r = (lane_r >> 6) * 16 + ((lane_r >> 2) & 7) * 2 + ((lane_r >> 5) & 1)
+    slot_r = iota((128, 128), 0)
+    key_r = ((slot_r >> 6) * 16 + ((slot_r >> 2) & 7) * 2 + ((slot_r >> 5) & 1)) * 4 + (slot_r & 3)
     for a in range(8):
-        owner, rank, held = held_steps(a)
-        selr += tn(((owner == owner_r) & (rank == (lane_r & 3))).astype(BF16), held)
+        key, held = held_steps(a)
+        selr += nt((key == key_r).astype(BF16), held)
     fetches[3].wait()
     rsend[...] = nt(selr.astype(BF16), res_ref[...]).astype(BF16)
     fetches[4].wait()
@@ -434,9 +436,7 @@
 
     for d in (4, 3, 5, 2, 6, 1, 7):
         send(ph.at[chip_rows(lax.rem(chip + d, 8))], rb.at[chip], p_s.at[d], p_r.at[d], tdev(2 * d))
-    fetches[7].wait()
     weight_send(1, 1)
-    weight_send(1, 2)
     total = ph[chip_rows(chip)].astype(F32)
     for d in range(1, 8):
         src = lax.rem(chip + 8 - d, 8)
@@ -463,8 +463,9 @@
         col = iota((128, 384), 1)
         pre = jnp.where(col == 320, sq_hi, jnp.where(col == 321, squares - sq_hi, pre))
         yb[rows] = pre.astype(BF16)
-        for m in range(4):
-            k = first_owner + m
+        nearby = pair // 4 == first_owner // 4
+        for far, near in ((0, 2), (1, 3), (3, 1), (2, 0)):
+            k = first_owner + lax.rem(pair + jnp.where(nearby, near, far), 4)
             piece = yb.at[pl.ds(pl.multiple_of(k * STEPS, STEPS), STEPS)]
 
             @pl.when(k != pair)
@@ -501,21 +502,21 @@
     col = iota((STEPS, 384), 1)
     squares = jnp.sum(jnp.where((col == 320) | (col == 321), total, 0.0), axis=1, keepdims=True)
     pre = jnp.where(col < 320, total * lax.rsqrt(squares / D + 1e-06), 0.0)
-    arrived(ob_z, o_r.at[0])
-    either(ob_z, ob, o_s.at[1], o_r.at[1], out_t)
     hidden = (pre / (1.0 + jnp.exp(-pre))).astype(BF16)
     fb[...] = nt(lwt[...], hidden)
     for d in range(1, 16):
         to_t = lax.rem(t + d, 16)
         send(fb.at[pl.ds(pl.multiple_of(to_t * 8, 8), 8)], fr.at[t], f_s.at[d], f_r.at[d], tdev(d))
-    arrived(ob, o_r.at[1])
-    states_ref[...] = ob[...]
+    arrived(ob_z, o_r.at[0])
+    either(ob_z, ob, o_s.at[1], o_r.at[1], out_t)
     total = fb[pl.ds(pl.multiple_of(t * 8, 8), 8)]
     for d in range(1, 16):
         src_t = lax.rem(t + 16 - d, 16)
         arrived(fr.at[src_t], f_r.at[d])
         total += fr[src_t]
     levels_ref[...] = total
+    arrived(ob, o_r.at[1])
+    states_ref[...] = ob[...]
 
     for copy in sends:
         copy.wait_send()
@@ -585,7 +586,7 @@
         out_specs=(vmem, vmem, vmem),
         scratch_shapes=scratch,
         compiler_params=pltpu.CompilerParams(
-            collective_id=0, has_side_effects=True, vmem_limit_bytes=56 * 1024 * 1024
+            collective_id=0, has_side_effects=True, vmem_limit_bytes=(54 * 1024 - 256) * 1024
         ),
     )(q, k, v, res.T, wo.T, gain, wm, lw, positions.reshape(8, 128))
     return attended, states, levels.T

time: 91.8 us -> 91.1 us (level)
  Pallas kernels: 88.2 us -> 86.9 us
    pallas_call x1, Pallas kernels: 88.2 us -> 86.9 us  [on_device(): pl.pallas_call(kernel, out_shape=(jax.ShapeDtypeStruct((TOK, 2 * HD), BF1...]
    unnamed x7 -> x9, local copies, waits for them, and re-layouts: 2.76 us -> 3.35 us
where the time goes in v4:
time: 91.1 us; the launch traced here: 90.9 us
  Pallas kernels  86.9 us (95%)
  local copies, waits for them, and re-layouts  3.35 us (4%)
    pallas_call x1, Pallas kernels, on_device(): pl.pallas_call(kernel, out_shape=(jax.ShapeDtypeStruct((TOK, 2 * HD), BF1...  86.9 us
    unnamed x9, local copies, waits for them, and re-layouts  3.35 us

profile of v4, /device:TPU:1, one launch (start us, length us, event | category | flops | bytes accessed | tf_op | source)
XLA Modules:
  0.0 90.9 jit_solution(16063051905504751547)
XLA Ops:
  0.6 0.0 copy-start.1
  0.6 0.0 copy-start.2
  0.7 0.7 copy-done.1
  1.3 0.0 copy-done.2
  1.3 0.0 copy-start
  1.3 0.8 copy-done
  2.2 86.9 %shard_map.112 = (bf16[128,256]{1,0:T(8,128)(2,1)S(1)}, bf16[32,320]{1,0:T(8,128)(2,1)S(1)}, f32[8,32]{1,0:T(8,128)S(1)}) custom-call(bf16[128,256]{1,0:T(8,128)(2,1)S(1)} %copy-done, bf16[128,1024]{1,0:T(8,128)(2,1)} %k_hbm.1, bf16[128,1024]{1,0:T(8,128)(2,1)} %v_hbm.1, bf16[320,128]{1,0:T(8,128)(2,1)} %bitcast.6, bf16[160,256]{1,0:T(8,128)(2,1)} %bitcast.7, ...), custom_call_target="tpu_custom_call" | custom-call | tf_op jit(solution)/shard_map/pallas_call | solution.py:578
  89.0 0.6 copy.15
  89.7 0.6 copy.16
  90.3 0.6 copy.17
Async XLA Ops:
  0.6 0.7 copy-start.1
  0.6 0.7 copy-start.2
  1.3 0.8 copy-start

commit v5 on v4

--- a/solution.py
+++ b/solution.py
@@ -377,6 +377,7 @@
             arrived(kv_block(1, n, f), near_r.at[1, n, f])
         kv_core(1, n)
 
+    weight_send(1, 1)
     for bundle in ((0, 1), (0, 2), (1, 1)):
         attend(*bundle)
     for f in range(4):
@@ -394,6 +395,8 @@
     for h in range(2):
         att_ref[:, h * HD : (h + 1) * HD] = mixed[h * 160 : h * 160 + TOK]
 
+    weight_wait(1, 1)
+    weight_send(1, 3)
     for d in range(1, 16):
         src_t = lax.rem(t + 16 - d, 16)
         arrived(gbuf.at[src_t], g_r.at[d])
@@ -436,7 +439,9 @@
 
     for d in (4, 3, 5, 2, 6, 1, 7):
         send(ph.at[chip_rows(lax.rem(chip + d, 8))], rb.at[chip], p_s.at[d], p_r.at[d], tdev(2 * d))
-    weight_send(1, 1)
+    weight_wait(1, 2)
+    weight_wait(1, 3)
+    wmbig[...] = nn(wmb[...], shift(320, 384, 0)).astype(BF16)
     total = ph[chip_rows(chip)].astype(F32)
     for d in range(1, 8):
         src = lax.rem(chip + 8 - d, 8)
@@ -446,14 +451,9 @@
     sb[own_rows] = total.astype(BF16)
     for d in (4, 3, 5, 2, 6, 1, 7):
         send(sb.at[own_rows], sb.at[own_rows], s_s.at[d], s_r.at[d], tdev(2 * d))
-    weight_wait(1, 1)
-    weight_send(1, 3)
-    weight_wait(1, 2)
     for d in range(1, 8):
         arrived(sb.at[chip_rows(core * 8 + lax.rem(chip + 8 - d, 8))], s_r.at[d])
     send(sb.at[mine], sb.at[mine], x_s.at[1], x_r.at[1], other_core)
-    weight_wait(1, 3)
-    wmbig[...] = nn(wmb[...], shift(320, 384, 0)).astype(BF16)
 
     def score(rows, first_owner):
         states = sb[rows].astype(F32)

time: 91.1 us -> 89.5 us (0.982)
  Pallas kernels: 86.9 us -> 85.3 us
    pallas_call x1, Pallas kernels: 86.9 us -> 85.3 us  [on_device(): pl.pallas_call(kernel, out_shape=(jax.ShapeDtypeStruct((TOK, 2 * HD), BF1...]
where the time goes in v5:
time: 89.5 us; the launch traced here: 89.3 us
  Pallas kernels  85.3 us (95%)
  local copies, waits for them, and re-layouts  3.35 us (4%)
    pallas_call x1, Pallas kernels, on_device(): pl.pallas_call(kernel, out_shape=(jax.ShapeDtypeStruct((TOK, 2 * HD), BF1...  85.3 us
    unnamed x9, local copies, waits for them, and re-layouts  3.35 us

profile of v5, /device:TPU:1, one launch (start us, length us, event | category | flops | bytes accessed | tf_op | source)
XLA Modules:
  0.0 89.3 jit_solution(11087203710659310865)
XLA Ops:
  0.6 0.0 copy-start.1
  0.6 0.0 copy-start.2
  0.7 0.7 copy-done.1
  1.3 0.0 copy-done.2
  1.3 0.0 copy-start
  1.3 0.8 copy-done
  2.2 85.3 %shard_map.112 = (bf16[128,256]{1,0:T(8,128)(2,1)S(1)}, bf16[32,320]{1,0:T(8,128)(2,1)S(1)}, f32[8,32]{1,0:T(8,128)S(1)}) custom-call(bf16[128,256]{1,0:T(8,128)(2,1)S(1)} %copy-done, bf16[128,1024]{1,0:T(8,128)(2,1)} %k_hbm.1, bf16[128,1024]{1,0:T(8,128)(2,1)} %v_hbm.1, bf16[320,128]{1,0:T(8,128)(2,1)} %bitcast.6, bf16[160,256]{1,0:T(8,128)(2,1)} %bitcast.7, ...), custom_call_target="tpu_custom_call" | custom-call | tf_op jit(solution)/shard_map/pallas_call | solution.py:578
  87.5 0.6 copy.15
  88.1 0.6 copy.16
  88.7 0.6 copy.17
Async XLA Ops:
  0.6 0.7 copy-start.1
  0.6 0.7 copy-start.2
  1.3 0.8 copy-start

commit v6 on v5

--- a/solution.py
+++ b/solution.py
@@ -272,8 +272,16 @@
     fetches[4].wait()
     either(rsend, rmid, m_s, m_r, res_mid)
     gbuf[t] = jnp.broadcast_to(gain_ref[...].astype(F32).reshape(1, 320), (16, 320)).astype(BF16)
-    for d in range(1, 16):
-        send(gbuf.at[t], gbuf.at[t], g_s.at[d], g_r.at[d], tdev(d))
+    gain_wanted = slot_t == pair
+
+    @pl.when(gain_wanted)
+    def _():
+        for d in range(1, 16):
+            pltpu.make_async_remote_copy(
+                src_ref=gbuf.at[t], dst_ref=gbuf.at[t], send_sem=g_s.at[d], recv_sem=g_r.at[half_t],
+                device_id=tdev(d), device_id_type=MESH,
+            ).start()
+
     fetches[5].wait()
     lwt[...] = nn(nt(eye128, lw_ref[...]).astype(BF16), shift(320, 384, 0)).astype(BF16)
 
@@ -397,9 +405,12 @@
 
     weight_wait(1, 1)
     weight_send(1, 3)
-    for d in range(1, 16):
-        src_t = lax.rem(t + 16 - d, 16)
-        arrived(gbuf.at[src_t], g_r.at[d])
+    for j in range(2):
+
+        @pl.when(t != j * 8 + pair)
+        def _(j=j):
+            arrived(gbuf.at[j * 8 + pair], g_r.at[j])
+
     gain = nn(gbuf[pair], shift(320, COLS, 0)) + nn(gbuf[8 + pair], shift(320, COLS, 320))
     gain = gain[0:1]
     for j in range(2):
@@ -520,6 +531,12 @@
 
     for copy in sends:
         copy.wait_send()
+
+    @pl.when(gain_wanted)
+    def _():
+        for d in range(1, 16):
+            arrived(gbuf.at[t], g_s.at[d])
+
     either_sent(rsend, m_s, res_mid)
     for g in range(4):
         either_sent(rmid.at[pl.ds(g * 32, 32)], r_s.at[g], res_dest(g))

time: 89.5 us -> 89.6 us (level)
  no operation moved by 1% of the time
where the time goes in v6:
time: 89.6 us; the launch traced here: 89.4 us
  Pallas kernels  85.3 us (95%)
  local copies, waits for them, and re-layouts  3.35 us (4%)
    pallas_call x1, Pallas kernels, on_device(): pl.pallas_call(kernel, out_shape=(jax.ShapeDtypeStruct((TOK, 2 * HD), BF1...  85.3 us
    unnamed x9, local copies, waits for them, and re-layouts  3.35 us

profile of v6, /device:TPU:1, one launch (start us, length us, event | category | flops | bytes accessed | tf_op | source)
XLA Modules:
  0.0 89.4 jit_solution(7573026350699989587)
XLA Ops:
  0.6 0.0 copy-start.1
  0.6 0.0 copy-start.2
  0.7 0.7 copy-done.1
  1.3 0.0 copy-done.2
  1.3 0.0 copy-start
  1.3 0.8 copy-done
  2.2 85.3 %shard_map.112 = (bf16[128,256]{1,0:T(8,128)(2,1)S(1)}, bf16[32,320]{1,0:T(8,128)(2,1)S(1)}, f32[8,32]{1,0:T(8,128)S(1)}) custom-call(bf16[128,256]{1,0:T(8,128)(2,1)S(1)} %copy-done, bf16[128,1024]{1,0:T(8,128)(2,1)} %k_hbm.1, bf16[128,1024]{1,0:T(8,128)(2,1)} %v_hbm.1, bf16[320,128]{1,0:T(8,128)(2,1)} %bitcast.6, bf16[160,256]{1,0:T(8,128)(2,1)} %bitcast.7, ...), custom_call_target="tpu_custom_call" | custom-call | tf_op jit(solution)/shard_map/pallas_call | solution.py:595
  87.5 0.6 copy.15
  88.2 0.6 copy.16
  88.8 0.6 copy.17
Async XLA Ops:
  0.6 0.7 copy-start.1
  0.6 0.7 copy-start.2
  1.3 0.8 copy-start
